TPU v7x, 256 devices: a whole 4x4x8 slice. The times are simulated.
256 devices in a mesh: gx: 32 (over z, y), gy: 8 (over x, core).
Axes of the slice: x: 4, y: 4, z: 8, core: 2. Of those that a mesh axis runs over, the one named last changes fastest.
Arguments:
- sources: bfloat16 [1, 64, 32, 64, 128], P(None, None, 'gx', 'gy'), may hold values from -6 to 6
- generator_weight: bfloat16 [3, 3, 3, 64, 64], replicated, may hold values from -0.4375 to 0.4375
- critic_kernel_weight: bfloat16 [3, 3, 3, 64, 64], replicated, may hold values from -0.15625 to 0.15625
- readout: float32 [64], replicated, may hold values from -1.5 to 1.5
- load_weight: int32 [32, 64], P('gx', 'gy'), may hold values from 1 to 8
Outputs:
- score: float32 [], replicated
- source_gradient: float32 [1, 64, 32, 64, 128], P(None, None, 'gx', 'gy')
- grad_gen: float32 [3, 3, 3, 64, 64], replicated
- grad_critic: float32 [3, 3, 3, 64, 64], replicated
All inputs are finite; a program needn't handle non-finite values.
Results may differ from a plain program's by a relative error of at most 0.0043.
Values may be sent and summed in bfloat16 or wider, within the bound.
A program may use at most 128 MiB of HBM per device.

v0:
```python
import math

import jax
import jax.numpy as jnp
from jax import lax
from jax.sharding import PartitionSpec as P

DIMS_SPEC = ("NCDHW", "DHWIO", "NCDHW")
SWAP_SPEC = ("CNDHW", "IODHW", "NCDHW")
LOG_TWO = 0.6931471805599453


def passed_along(value, axis, steps):
    count = lax.axis_size(axis)
    first, last = (max(0, -steps), min(count, count - steps))
    return lax.ppermute(value, axis, [(source, source + steps) for source in range(first, last)])


def activation(value):
    return 0.2 * value + 0.8 * (jax.nn.softplus(value) - LOG_TWO)


def act_slope(value):
    return 0.2 + 0.8 * jax.nn.sigmoid(value)


def upsample(source_field, kernel_taps, planar_padding):
    return lax.conv_general_dilated(
        source_field,
        jnp.flip(kernel_taps, (0, 1, 2)),
        (1, 1, 1),
        [planar_padding, planar_padding, (1, 2)],
        lhs_dilation=(2, 2, 2),
        dimension_numbers=DIMS_SPEC,
        preferred_element_type=jnp.float32,
    )


def coarsen_field(source_field, kernel_taps, planar_padding):
    return lax.conv_general_dilated(
        source_field,
        kernel_taps,
        (2, 2, 2),
        [planar_padding, planar_padding, (1, 0)],
        dimension_numbers=DIMS_SPEC,
        preferred_element_type=jnp.float32,
    )


def gen_taps(upper_box, grad_out):
    taps_out = lax.conv_general_dilated(
        grad_out,
        upper_box,
        (1, 1, 1),
        [(1, 2), (1, 2), (1, 0)],
        rhs_dilation=(2, 2, 2),
        dimension_numbers=SWAP_SPEC,
        preferred_element_type=jnp.float32,
    )
    return jnp.transpose(taps_out, (2, 3, 4, 1, 0))


def critic_taps(lower_bounding_box, grad_out):
    taps_out = lax.conv_general_dilated(
        lower_bounding_box,
        grad_out,
        (1, 1, 1),
        [(0, 0), (0, 0), (1, 0)],
        rhs_dilation=(2, 2, 2),
        dimension_numbers=SWAP_SPEC,
        preferred_element_type=jnp.float32,
    )
    return jnp.transpose(taps_out, (2, 3, 4, 0, 1))


def extend_halo(source_field, step_dir):
    edge_layer = source_field[:, :, :1] if step_dir < 0 else source_field[:, :, -1:]
    arrived = passed_along(edge_layer, "gx", step_dir)
    source_field = jnp.concatenate(
        [source_field, arrived] if step_dir < 0 else [arrived, source_field], 2
    )
    edge_layer = source_field[:, :, :, :1] if step_dir < 0 else source_field[:, :, :, -1:]
    arrived = passed_along(edge_layer, "gy", step_dir)
    return jnp.concatenate([source_field, arrived] if step_dir < 0 else [arrived, source_field], 3)


def shards(sources, generator_weight, critic_kernel_weight, readout, load_weight):
    upper_box = extend_halo(sources, -1)
    pre_gen = upsample(upper_box, generator_weight, (1, 0))
    lower_bounding_box = extend_halo(activation(pre_gen).astype(jnp.bfloat16), 1)
    critic_preactivation = coarsen_field(lower_bounding_box, critic_kernel_weight, (0, 0))
    col_weight = load_weight.astype(jnp.float32)[None, :, :, None]
    read_col = readout[None, :, None, None, None]
    logits = jnp.sum(activation(critic_preactivation) * read_col, 1)
    loss_sum = jnp.sum(col_weight * jax.nn.softplus(-logits))
    d_logit = -col_weight * jax.nn.sigmoid(-logits)
    d_critic = (d_logit[:, None] * read_col * act_slope(critic_preactivation)).astype(jnp.bfloat16)
    crit_grad = critic_taps(lower_bounding_box, d_critic)
    back_kernel = jnp.swapaxes(critic_kernel_weight, 3, 4)
    d_field = upsample(extend_halo(d_critic, -1), back_kernel, (1, 0))
    generator_gradient = (d_field * act_slope(pre_gen)).astype(jnp.bfloat16)
    gen_grad = gen_taps(upper_box, generator_gradient)
    source_gradient = coarsen_field(
        extend_halo(generator_gradient, 1), jnp.swapaxes(generator_weight, 3, 4), (0, 0)
    )
    total_loss, total_gen, total_crit = lax.psum((loss_sum, gen_grad, crit_grad), ("gx", "gy"))
    shape_in = sources.shape
    cell_count = (
        shape_in[0]
        * shape_in[2]
        * shape_in[3]
        * shape_in[4]
        * lax.axis_size("gx")
        * lax.axis_size("gy")
    )
    root = 1.0 / math.sqrt(cell_count)
    return (total_loss / cell_count, source_gradient, total_gen * root, total_crit * root)


def solution(mesh):
    placed = (P(None, None, "gx", "gy", None), P(), P(), P(), P("gx", "gy"))
    return jax.shard_map(
        shards,
        mesh=mesh,
        in_specs=placed,
        out_specs=(P(), P(None, None, "gx", "gy", None), P(), P()),
        check_vma=False,
    )
```

profile of v0, /device:TPU:1, one launch (start us, length us, event | category | flops | bytes accessed | tf_op | source)
XLA Modules:
  0.0 556.1 jit_solution(10427570710697901100)
XLA Ops:
  7.2 1.4 collective-permute-start
  9.6 4.4 collective-permute-done
  14.0 5.6 %collective-permute-start.1 = (bf16[1,64,2,1,128]{4,3,2,1,0:T(2,128)(2,1)S(1)}, bf16[1,64,2,1,128]{4,3,2,1,0:T(2,128)(2,1)S(1)}, u32[]{:S(2)}, u32[]{:S(2)}) collective-permute-start(bf16[1,64,2,1,128]{4,3,2,1,0:T(2,128)(2,1)S(1)} %slice.41), channel_id=1, source_target_pairs={{1,0},{2,1},{3,2},{4,3},{5,4},{6,5},{7,6},{9,8},{10,9},{11,10},{12... | collective-permute-start | bytes 98312 | tf_op jit(solution)/shard_map/ppermute | solution.py:16
  19.7 1.6 collective-permute-done.1
  23.8 6.1 %fusion.7 = (bf16[2,16,8,34,64]{4,2,3,1,0:T(8,128)(2,1)S(1)}, f32[2,16,8,34,64]{4,2,3,1,0:T(8,128)}) fusion(pred[8,34]{0,1:T(8,128)(4,1)S(1)} %copy-done.5, bf16[3,3,3,64,64]{4,3,2,1,0:T(8,128)(2,1)S(1)} %copy-done, bf16[64,2,9,1,7,1]{0,4,5,2,1,3:T(8,128)(2,1)S(1)} %slice.42, bf16[64,2,9,1,8,17]{0,4,5,2,1,3:T(8,128)(2,1)S(1)} %copy.160), kind=kOutput, calls=%fused_computation.11 | convolution fusion | flops 248328192 | bytes 3893264 | tf_op jit(solution)/shard_map/conv_general_dilated | solution.py:28
  30.3 1.2 slice_bitcast_fusion.2
  31.5 2.6 copy.162
  34.1 4.0 collective-permute-start.2
  39.1 6.4 %copy.213 = bf16[2,16,1,256,64]{4,2,3,1,0:T(2,128)(2,1)} copy(bf16[2,16,1,256,64]{4,1,3,0,2:T(8,128)(2,1)S(1)} %slice.45) | data formatting | bytes 2097152
  45.5 2.2 collective-permute-done.2
  47.7 3.2 copy.165
  50.9 1.7 pad_maximum_fusion.3
  52.6 3.9 collective-permute-start.3
  56.5 4.2 collective-permute-done.3
  60.8 12.9 %maximum_maximum_fusion = bf16[1,64,3,17,256]{1,0,4,3,2:T(2,128)(2,1)} fusion(bf16[1,64,2,16,256]{1,0,4,3,2:T(2,128)(2,1)S(1)} %bitcast.98, bf16[1,64,1,16,256]{1,0,4,3,2:T(2,128)(2,1)S(1)} %copy.165, bf16[1,64,3,1,256]{1,0,4,3,2:T(2,128)(2,1)S(1)} %collective-permute-done.3), kind=kLoop, calls=%fused_computation.4 | loop fusion | flops 1671168 | bytes 3342336 | tf_op jit(solution)/shard_map/concatenate | solution.py:84
  73.6 15.3 %copy.166 = bf16[1,64,3,17,256]{4,1,3,2,0:T(8,128)(2,1)} copy(bf16[1,64,3,17,256]{1,0,4,3,2:T(2,128)(2,1)} %maximum_maximum_fusion) | data formatting | bytes 3342336 | tf_op jit(solution)/shard_map/concatenate | solution.py:84
  89.0 2.6 pad.2
  91.6 7.3 %reshape.194 = bf16[64,3,17,1,8,34]{5,4,0,2,1,3:T(8,128)(2,1)} reshape(bf16[64,3,17,1,272]{4,0,3,2,1:T(8,128)(2,1)S(1)} %pad.2) | data formatting | bytes 3551232 | tf_op jit(solution)/shard_map/conv_general_dilated | solution.py:40
  98.9 10.1 %copy.169 = bf16[64,3,17,1,8,34]{0,4,5,2,1,3:T(8,128)(2,1)} copy(bf16[64,3,17,1,8,34]{5,4,0,2,1,3:T(8,128)(2,1)} %reshape.194) | data formatting | bytes 3551232 | tf_op jit(solution)/shard_map/conv_general_dilated | solution.py:40
  110.0 3.8 multiply_add_fusion
  114.7 1.3 collective-permute-start.4
  116.6 16.7 %fusion.57 = f32[3,3,3,64,64]{3,4,2,1,0:T(8,128)} fusion(bf16[1,64,3,17,256]{1,0,4,3,2:T(2,128)(2,1)} %maximum_maximum_fusion, bf16[1,64,1,8,128]{1,3,4,0,2:T(8,128)(2,1)S(1)} %fusion.56), kind=kOutput, calls=%fused_computation.73 | convolution fusion | flops 225902592 | bytes 2244608 | tf_op jit(solution)/shard_map/transpose | solution.py:73
  133.3 85.1 %psum.21 = f32[]{:T(128)} all-reduce(f32[]{:T(128)} %fusion.64), channel_id=1, replica_groups=mesh['gx'=32,'gy'=8] {'gx','gy'}, use_global_device_ids=true, to_apply=%region_2.3 | all-reduce | flops 1 | bytes 8 | tf_op jit(solution)/shard_map/psum | solution.py:106
  219.3 2.7 collective-permute-start.5
  222.5 3.1 collective-permute-done.5
  227.2 4.6 multiply_convert_fusion
  231.8 1.7 fusion.22
  234.2 1.3 copy.179
  235.5 2.5 fusion.19
  238.0 8.0 %fusion.28 = f32[3,3,3,64,64]{3,4,2,1,0:T(8,128)} fusion(bf16[64,2,9,8,17,1]{0,1,4,3,2,5:T(2,128)(2,1)S(1)} %bitcast.105, bf16[2,16,8,34,64,1]{4,2,3,1,0,5:T(8,128)(2,1)} %get-tuple-element.40, bf16[2,16,8,34,64,1]{4,2,3,1,0,5:T(8,128)(2,1)} %get-tuple-element.30, bf16[2,16,8,34,64,1]{4,2,3,1,0,5:T(8,128)(2,1)} %get-tuple-element.41), kind=kOutput, calls=%fused_computation.42 | convolution fusion | flops 243990528 | bytes 4098048 | tf_op jit(solution)/shard_map/transpose | solution.py:60
  246.1 2.4 slice_bitcast_fusion.1
  248.4 1.9 copy.181
  250.4 3.4 copy.180
  253.8 3.3 collective-permute-start.6
  257.1 2.0 slice_bitcast_fusion
  259.1 241.9 %all-reduce.3.cloned.1.call-done = (f32[3,3,3,64,64]{3,4,2,1,0:T(8,128)}, f32[3,3,3,64,64]{3,4,2,1,0:T(8,128)}) async-done(((f32[3,3,3,64,64]{3,4,2,1,0:T(8,128)}, f32[3,3,3,64,64]{3,4,2,1,0:T(8,128)}), (f32[3,3,3,64,64]{3,4,2,1,0:T(8,128)}, f32[3,3,3,64,64]{3,4,2,1,0:T(8,128)})) %all-reduce.3.cloned.1.call-update) | async-done | bytes 884752 | tf_op jit(solution)/shard_map/psum | solution.py:106
  500.9 1.2 broadcast_multiply_fusion.1
  502.2 1.2 copy.195
  503.4 1.2 broadcast_multiply_fusion
  504.6 1.2 copy.196
  505.8 3.6 copy.182
  509.4 1.8 fusion.59
  511.2 5.4 collective-permute-start.7
  516.7 2.3 pad_maximum_fusion.1
  518.9 4.0 copy.184
  524.6 7.2 %reshape.195 = bf16[64,3,17,1,8,34]{5,4,0,2,1,3:T(8,128)(2,1)} reshape(bf16[64,3,17,1,272]{4,0,2,1,3:T(8,128)(2,1)S(1)} %pad.9) | data formatting | bytes 3551232 | tf_op jit(solution)/shard_map/conv_general_dilated | solution.py:40
  531.7 10.0 %copy.187 = bf16[64,3,17,1,8,34]{0,4,5,2,1,3:T(8,128)(2,1)} copy(bf16[64,3,17,1,8,34]{5,4,0,2,1,3:T(8,128)(2,1)} %reshape.195) | data formatting | bytes 3551232 | tf_op jit(solution)/shard_map/conv_general_dilated | solution.py:40
  542.7 4.1 fusion.34
  (69 shorter events, 14.0 us)
Async XLA Ops:
  7.2 16.7 %copy-start = (bf16[3,3,3,64,64]{4,3,2,1,0:T(8,128)(2,1)S(1)}, bf16[3,3,3,64,64]{4,3,2,1,0:T(8,128)(2,1)}, u32[]{:S(2)}) copy-start(bf16[3,3,3,64,64]{4,3,2,1,0:T(8,128)(2,1)} %param.6) | copy-start | bytes 663556
  7.2 16.6 %copy-start.5 = (pred[8,34]{0,1:T(8,128)(4,1)S(1)}, pred[8,34]{0,1:T(8,128)(4,1)}, u32[]{:S(2)}) copy-start(pred[8,34]{0,1:T(8,128)(4,1)} %constant.52) | copy-start | bytes 820
  7.2 493.7 %all-reduce.3.cloned.1.call-start = ((), (), s32[]{:S(2)}) async-start(), calls=%async_computation | async-start | bytes 3538944 | tf_op jit(solution)/shard_map/psum | solution.py:106
  7.2 6.7 %collective-permute-start = (bf16[1,64,1,8,128]{4,3,2,1,0:T(8,128)(2,1)}, bf16[1,64,1,8,128]{4,3,2,1,0:T(8,128)(2,1)S(1)}, u32[]{:S(2)}, u32[]{:S(2)}) collective-permute-start(bf16[1,64,1,8,128]{4,3,2,1,0:T(8,128)(2,1)} %param.5), channel_id=1, source_target_pairs={{8,0},{16,8},{24,16},{32,24},{40,32},{48,40},{56,48},{64,56},{72,6... | collective-permute-start | bytes 393224 | tf_op jit(solution)/shard_map/ppermute | solution.py:16
  14.0 7.2 %collective-permute-start.1 = (bf16[1,64,2,1,128]{4,3,2,1,0:T(2,128)(2,1)S(1)}, bf16[1,64,2,1,128]{4,3,2,1,0:T(2,128)(2,1)S(1)}, u32[]{:S(2)}, u32[]{:S(2)}) collective-permute-start(bf16[1,64,2,1,128]{4,3,2,1,0:T(2,128)(2,1)S(1)} %slice.41), channel_id=1, source_target_pairs={{1,0},{2,1},{3,2},{4,3},{5,4},{6,5},{7,6},{9,8},{10,9},{11,10},{12... | collective-permute-start | bytes 98312 | tf_op jit(solution)/shard_map/ppermute | solution.py:16
  23.0 0.8 copy-start.3
  29.9 8.2 %copy-start.9 = (s32[1,8]{1,0:T(1,128)S(1)}, s32[1,8]{1,0:T(1,128)}, u32[]{:S(2)}) copy-start(s32[1,8]{1,0:T(1,128)} %param.9) | copy-start | bytes 100
  34.1 13.6 %collective-permute-start.2 = (bf16[1,64,1,16,256]{4,3,2,1,0:T(8,128)(2,1)S(1)}, bf16[1,64,1,16,256]{4,3,2,1,0:T(8,128)(2,1)}, u32[]{:S(2)}, u32[]{:S(2)}) collective-permute-start(bf16[1,64,1,16,256]{4,3,2,1,0:T(8,128)(2,1)S(1)} %copy.162), channel_id=1, source_target_pairs={{0,8},{8,16},{16,24},{24,32},{32,40},{40,48},{48,56},{56,64},{64,7... | collective-permute-start | bytes 1572872 | tf_op jit(solution)/shard_map/ppermute | solution.py:16
  50.9 9.9 %copy-start.1 = (bf16[2,16,1,256,64]{4,2,3,1,0:T(2,128)(2,1)S(1)}, bf16[2,16,1,256,64]{4,2,3,1,0:T(2,128)(2,1)}, u32[]{:S(2)}) copy-start(bf16[2,16,1,256,64]{4,2,3,1,0:T(2,128)(2,1)} %copy.213) | copy-start | bytes 3145732
  52.6 8.1 %collective-permute-start.3 = (bf16[1,64,3,1,256]{1,0,4,3,2:T(2,128)(2,1)S(1)}, bf16[1,64,3,1,256]{1,0,4,3,2:T(2,128)(2,1)S(1)}, u32[]{:S(2)}, u32[]{:S(2)}) collective-permute-start(bf16[1,64,3,1,256]{1,0,4,3,2:T(2,128)(2,1)S(1)} %pad_maximum_fusion.3), channel_id=1, source_target_pairs={{0,1},{1,2},{2,3},{3,4},{4,5},{5,6},{6,7},{8,9},{9,10},{10,11},{11... | collective-permute-start | bytes 294920 | tf_op jit(solution)/shard_map/ppermute | solution.py:16
  98.9 11.1 %copy-start.6 = (f32[64]{0:T(128)S(1)}, f32[64]{0:T(128)}, u32[]{:S(2)}) copy-start(f32[64]{0:T(128)} %param.8) | copy-start | bytes 772
  98.9 11.1 %copy-start.7 = (bf16[3,3,3,64,64]{4,3,2,1,0:T(8,128)(2,1)S(1)}, bf16[3,3,3,64,64]{4,3,2,1,0:T(8,128)(2,1)}, u32[]{:S(2)}) copy-start(bf16[3,3,3,64,64]{4,3,2,1,0:T(8,128)(2,1)} %param.7) | copy-start | bytes 663556
  98.9 11.1 %copy-start.10 = (pred[8,17]{0,1:T(8,128)(4,1)S(1)}, pred[8,17]{0,1:T(8,128)(4,1)}, u32[]{:S(2)}) copy-start(pred[8,17]{0,1:T(8,128)(4,1)} %constant.51) | copy-start | bytes 412
  114.7 104.4 %collective-permute-start.4 = (bf16[1,64,1,8,128]{1,3,4,0,2:T(8,128)(2,1)S(1)}, bf16[1,64,1,8,128]{1,3,4,0,2:T(8,128)(2,1)S(1)}, u32[]{:S(2)}, u32[]{:S(2)}) collective-permute-start(bf16[1,64,1,8,128]{1,3,4,0,2:T(8,128)(2,1)S(1)} %fusion.56), channel_id=1, source_target_pairs={{8,0},{16,8},{24,16},{32,24},{40,32},{48,40},{56,48},{64,56},{72,6... | collective-permute-start | bytes 393224 | tf_op jit(solution)/shard_map/ppermute | solution.py:16
  133.3 93.9 %copy-start.8 = (bf16[3,3,3,64,64]{4,3,2,1,0:T(8,128)(2,1)S(1)}, bf16[3,3,3,64,64]{4,3,2,1,0:T(8,128)(2,1)}, u32[]{:S(2)}) copy-start(bf16[3,3,3,64,64]{4,3,2,1,0:T(8,128)(2,1)} %param.7) | copy-start | bytes 663556
  219.3 6.3 %collective-permute-start.5 = (bf16[1,64,2,1,128]{1,3,4,0,2:T(2,128)(2,1)S(1)}, bf16[1,64,2,1,128]{1,3,4,0,2:T(2,128)(2,1)S(1)}, u32[]{:S(2)}, u32[]{:S(2)}) collective-permute-start(bf16[1,64,2,1,128]{1,3,4,0,2:T(2,128)(2,1)S(1)} %fusion.62), channel_id=1, source_target_pairs={{1,0},{2,1},{3,2},{4,3},{5,4},{6,5},{7,6},{9,8},{10,9},{11,10},{12... | collective-permute-start | bytes 98312 | tf_op jit(solution)/shard_map/ppermute | solution.py:16
  235.5 2.6 copy-start.4
  253.8 252.0 %collective-permute-start.6 = (bf16[1,64,1,16,256]{4,3,2,1,0:T(8,128)(2,1)}, bf16[1,64,1,16,256]{4,3,2,1,0:T(8,128)(2,1)}, u32[]{:S(2)}, u32[]{:S(2)}) collective-permute-start(bf16[1,64,1,16,256]{4,3,2,1,0:T(8,128)(2,1)} %copy.180), channel_id=1, source_target_pairs={{0,8},{8,16},{16,24},{24,32},{32,40},{40,48},{48,56},{56,64},{64,7... | collective-permute-start | bytes 1572872 | tf_op jit(solution)/shard_map/ppermute | solution.py:16
  509.4 7.3 %copy-start.2 = (bf16[1,64,1,16,256]{1,3,4,2,0:T(8,128)(2,1)S(1)}, bf16[1,64,1,16,256]{1,3,4,2,0:T(8,128)(2,1)}, u32[]{:S(2)}) copy-start(bf16[1,64,1,16,256]{1,3,4,2,0:T(8,128)(2,1)} %copy.182) | copy-start | bytes 1572868
  511.2 11.7 %collective-permute-start.7 = (bf16[1,64,3,1,256]{1,3,4,2,0:T(2,128)(2,1)S(1)}, bf16[1,64,3,1,256]{1,3,4,2,0:T(2,128)(2,1)S(1)}, u32[]{:S(2)}, u32[]{:S(2)}) collective-permute-start(bf16[1,64,3,1,256]{1,3,4,2,0:T(2,128)(2,1)S(1)} %fusion.59), channel_id=1, source_target_pairs={{0,1},{1,2},{2,3},{3,4},{4,5},{5,6},{6,7},{8,9},{9,10},{10,11},{11... | collective-permute-start | bytes 294920 | tf_op jit(solution)/shard_map/ppermute | solution.py:16
Sparse Core Ops, SparseCore 0:
  246.2 254.6 all-reduce.2
where the time goes:
time: 566 us; the launch traced here: 556 us
  waiting for transfers between devices  257 us (45%)
  local copies, waits for them, and re-layouts  99.1 us (18%)
  blocking collectives  85.1 us (15%)
  matrix products  43.2 us (8%)
  starting transfers between devices  27.7 us (5%)
  other arithmetic  27.2 us (5%)
  between operations  16.5 us (3%)
    psum x1, waiting for transfers between devices, shards(): lax.psum((loss_sum, gen_grad, crit_grad), ('gx', 'gy'))  242 us
    psum x1, blocking collectives, shards(): lax.psum((loss_sum, gen_grad, crit_grad), ('gx', 'gy'))  85.1 us
    conv_general_dilated x8, local copies, waits for them, and re-layouts, coarsen_field(): lax.conv_general_dilated(source_field, kernel_taps, (2, 2, 2), [planar_pa...  36.7 us
    ppermute x8, starting transfers between devices, passed_along(): lax.ppermute(value, axis, [(source, source + steps) for source in range(f...  27.7 us
    concatenate x8, local copies, waits for them, and re-layouts, extend_halo(): jnp.concatenate([source_field, arrived] if step_dir < 0 else [arrived, so...  24.7 us
    concatenate x9, other arithmetic, extend_halo(): jnp.concatenate([source_field, arrived] if step_dir < 0 else [arrived, so...  19.3 us
    transpose x1, matrix products, critic_taps(): return jnp.transpose(taps_out, (2, 3, 4, 0, 1))  16.7 us
    ppermute x8, waiting for transfers between devices, passed_along(): lax.ppermute(value, axis, [(source, source + steps) for source in range(f...  15.4 us
  transfers between devices with their start and end apart: 9, of which 6 were waited for; matrix products, arithmetic and copies ran while one was open for 8% of the time, Pallas kernels for 0%

commit v1 on v0

v1 whole, which is shorter than its diff:
```python
import math

import jax
import jax.numpy as jnp
from jax import lax
from jax.experimental import pallas as pl
from jax.experimental.pallas import tpu as pltpu
from jax.sharding import PartitionSpec as P

MESH = pl.DeviceIdType.MESH
BF = jnp.bfloat16
F32 = jnp.float32
ROWS = 10
LANES = ROWS * 128
TILES = 14
TAP = {(0, 0): 1, (1, 0): 2, (1, 1): 0}
SIDES = [(1, 0), (-1, 0), (0, 1), (0, -1), (1, 1), (1, -1), (-1, 1), (-1, -1)]


def dot(a, b):
    return lax.dot_general(a, b, (((1,), (0,)), ((), ())), preferred_element_type=F32)


def dot_t(a, b):
    return lax.dot_general(a, b, (((1,), (1,)), ((), ())), preferred_element_type=F32)


def lane(shape):
    return lax.broadcasted_iota(jnp.int32, shape, len(shape) - 1)


def next_z(value):
    moved = pltpu.roll(value, 127, 1)
    return jnp.where(lane(value.shape) < 127, moved, 0.0)


def prev_z(value):
    moved = pltpu.roll(value, 1, 1)
    return jnp.where(lane(value.shape) > 0, moved, 0.0)


def at(row, count=1):
    return pl.ds(pl.multiple_of(row * 128, 128), count * 128)


def split_round(value, holds_loss):
    plain = value.astype(BF)
    loss = value[0:16] + value[16:32] + value[32:48]
    high = loss.astype(BF)
    rest = loss - high.astype(F32)
    middle = rest.astype(BF)
    low = (rest - middle.astype(F32)).astype(BF)
    parts = jnp.concatenate([high, middle, low, jnp.zeros_like(high)], 0).astype(F32)
    use = jnp.logical_and(lane(value.shape) >= 64, holds_loss)
    return jnp.where(use, parts, plain.astype(F32)).astype(BF)


def kernel(
    src_ref, wg_ref, wc_ref, ro_ref, lw_ref,
    score_ref, sg_ref, gg_ref, gc_ref,
    stage, sbuf, dbuf, wg, wgt, wc, wct, u, d, f, slope, dg, q, ro, lossv,
    part, core_rx, psend, plane_rx, z_rx, fin,
    s_s, s_r, d_s, d_r, csem, p_s, p_r, z_s, z_r, g_s, g_r, f_s, f_r,
):
    gx, gy = lax.axis_index("gx"), lax.axis_index("gy")
    z, y, x, core = gx // 4, gx % 4, gy // 2, gy % 2
    pme = x * 4 + y

    def plane_dev(p):
        return (z * 4 + p % 4, (p // 4) * 2 + core)

    def z_dev(t):
        return (t * 4 + y, gy)

    core_dev = (gx, x * 2 + (1 - core))

    def side_dev(side):
        return ((gx + side[0] + 32) % 32, (gy + side[1] + 8) % 8)

    def rcopy(src, dst, send, recv, dev):
        return pltpu.make_async_remote_copy(
            src_ref=src, dst_ref=dst, send_sem=send, recv_sem=recv, device_id=dev, device_id_type=MESH
        )

    def halo(buf, n, send, recv):
        dx, dy = SIDES[n]
        here = pl.ds(1, 8) if dy == 0 else pl.ds(8 if dy > 0 else 1, 1)
        there = pl.ds(1, 8) if dy == 0 else pl.ds(0 if dy > 0 else 9, 1)
        return rcopy(buf.at[1, here], buf.at[1 - dx, there], send.at[n], recv.at[n], side_dev(SIDES[n]))

    barrier = pltpu.get_barrier_semaphore()

    def greet(dev):
        pl.semaphore_signal(barrier, inc=1, device_id=dev, device_id_type=MESH)

    for side in SIDES:
        greet(side_dev(side))
    greet(core_dev)

    @pl.loop(1, 16)
    def _(t):
        greet(plane_dev((pme + t) % 16))

    @pl.loop(1, 8)
    def _(t):
        greet(z_dev((z + t) % 8))

    stage[...] = src_ref[...].astype(F32)
    for r in range(8):
        sbuf[1, r + 1] = stage[:, r, :].astype(BF)

    pl.semaphore_wait(barrier, 8 + 1 + 15 + 7)
    for n in range(8):
        halo(sbuf, n, s_s, s_r).start()

    zero = jnp.zeros((64, 64), F32)
    for s in range(3):
        for ay in range(2):
            for az in range(2):
                rows = pl.ds((ay * 2 + az) * 64, 64)
                for by in range(2):
                    pair = []
                    for bz in range(2):
                        ok = (by, ay) in TAP and (bz, az) in TAP
                        pair.append(wg_ref[s * 9 + TAP[by, ay] * 3 + TAP[bz, az]].astype(F32) if ok else zero)
                    wg[s, rows, pl.ds(by * 128, 128)] = jnp.concatenate(pair, 1).astype(BF)
                    pair = []
                    for bz in range(2):
                        ok = (ay, by) in TAP and (az, bz) in TAP
                        pair.append(wc_ref[s * 9 + TAP[ay, by] * 3 + TAP[az, bz]].astype(F32) if ok else zero)
                    wc[s, rows, pl.ds(by * 128, 128)] = jnp.concatenate(pair, 1).astype(BF)
        wgt[s] = wg[s].astype(F32).T.astype(BF)
        wct[s] = wc[s].astype(F32).T.astype(BF)
    ro[...] = jnp.broadcast_to(ro_ref[...], (128, 64)).T

    def spread(buf, out, xs, r, keep=None):
        value = buf[xs, r].astype(F32)
        if keep is not None:
            value = jnp.where(keep, value, 0.0)
        return value.astype(BF), next_z(value).astype(BF)

    def put_here(out, xs, r, pair):
        out[xs, 0:64, at(r)] = pair[0]
        out[xs, 64:128, at(r)] = pair[1]

    def put_below(out, xs, r, pair):
        out[xs, 128:192, at(r - 1)] = pair[0]
        out[xs, 192:256, at(r - 1)] = pair[1]

    def clear(out, xs):
        nothing = jnp.zeros((128, 128), BF)
        out[xs, 0:128, at(0)] = nothing
        out[xs, 0:128, at(9)] = nothing
        out[xs, 128:256, at(8)] = nothing
        out[xs, 128:256, at(9)] = nothing

    def own_rows(buf, out, xs, keep=None):
        @pl.loop(1, 9)
        def _(r):
            pair = spread(buf, out, xs, r, keep)
            put_here(out, xs, r, pair)
            put_below(out, xs, r, pair)

    def edge_rows(buf, out, xs, keep=True):
        put_here(out, xs, 0, spread(buf, out, xs, 0, keep))
        put_below(out, xs, 9, spread(buf, out, xs, 9, jnp.logical_and(keep, gy < 7)))

    clear(u, 1)
    own_rows(sbuf, u, 1)
    clear(d, 1)

    for n in range(8):
        halo(sbuf, n, s_s, s_r).wait_recv()
    for xs in (0, 2):
        clear(u, xs)
    edge_rows(sbuf, u, 1)
    own_rows(sbuf, u, 0)
    edge_rows(sbuf, u, 0)
    own_rows(sbuf, u, 2, gx < 31)
    edge_rows(sbuf, u, 2, gx < 31)

    def up(weights, field, c):
        mid = field[1, :, c]
        return (
            dot(weights[2], field[0, :, c]) + dot(weights[0], mid),
            dot(weights[1], mid),
            dot(weights[2], mid) + dot(weights[0], field[2, :, c]),
        )

    @pl.loop(0, ROWS // 2)
    def _(i):
        c = at(i * 2, 2)
        for s, v in enumerate(up(wgt, u, c)):
            t = jnp.tanh(0.5 * v)
            f[s, :, c] = (jnp.maximum(v, 0.2 * v) - 0.8 * jnp.log(1.0 + jnp.abs(t))).astype(BF)
            slope[s, :, c] = 0.6 + 0.4 * t

    @pl.when(gx == 0)
    def _():
        f[0] = jnp.zeros((256, LANES), BF)
        slope[0] = jnp.zeros((256, LANES), F32)

    @pl.when(gy == 0)
    def _():
        for s in range(3):
            f[s, :, 0:128] = jnp.zeros((256, 128), BF)
            slope[s, :, 0:128] = jnp.zeros((256, 128), F32)

    def down(weights, field, c):
        return dot(weights[0], field[0, :, c]) + dot(weights[1], field[1, :, c]) + dot(weights[2], field[2, :, c])

    def gathered(r):
        near = q[0:64, at(r)] + q[128:192, at(r - 1)]
        far = q[64:128, at(r)] + q[192:256, at(r - 1)]
        return near + prev_z(far)

    @pl.loop(0, ROWS // 2)
    def _(i):
        c = at(i * 2, 2)
        q[:, c] = down(wct, f, c)

    lossv[...] = jnp.zeros((1, 128), F32)

    @pl.loop(1, 9)
    def _(r):
        v = gathered(r)
        t = jnp.tanh(0.5 * v)
        act = jnp.maximum(v, 0.2 * v) - 0.8 * jnp.log(1.0 + jnp.abs(t))
        logits = jnp.sum(act * ro[...], 0, keepdims=True)
        weight = lw_ref[0, r - 1].astype(F32)
        e = jnp.exp(-jnp.abs(logits))
        lossv[...] += weight * (jnp.maximum(-logits, 0.0) + jnp.log1p(e))
        d_logit = -weight * jnp.where(logits >= 0, e, 1.0) / (1.0 + e)
        dbuf[1, r] = (d_logit * ro[...] * (0.6 + 0.4 * t)).astype(BF)

    for n in range(8):
        halo(dbuf, n, d_s, d_r).start()
    own_rows(dbuf, d, 1)

    def pack(g, s, full, halves):
        for j in range(3):
            n = s * 3 + j
            part[g, n] = full[j]
            left = lane((64, 128)) < 64
            half = halves[j]
            if (g == 0) == (n % 2 == 1):
                half = pltpu.roll(half, 64, 1)
            if n % 2 == 0:
                part[g, 9 + n // 2] = jnp.where(left, half, 0.0)
            else:
                part[g, 9 + n // 2] = jnp.where(left, part[g, 9 + n // 2], half)

    for s in range(3):
        q[:, 0:256] = dot_t(f[s], d[1])
        pairs = [(0, 0), (1, 0), (1, 1)]
        pack(
            0, s,
            [q[(p * 2 + 1) * 64:(p * 2 + 2) * 64, e * 128:e * 128 + 128] for p, e in pairs],
            [q[p * 128:p * 128 + 64, e * 128:e * 128 + 128] for p, e in pairs],
        )
    loss = jnp.broadcast_to(jnp.sum(lossv[...], 1, keepdims=True), (16, 128))
    put = lane((16, 128)) >= 64
    part[0, 13, 0:16, :] = jnp.where(put, loss, part[0, 13, 0:16, :])

    for n in range(8):
        halo(dbuf, n, d_s, d_r).wait_recv()
    for xs in (0, 2):
        clear(d, xs)
    edge_rows(dbuf, d, 1)
    own_rows(dbuf, d, 0)
    edge_rows(dbuf, d, 0)
    own_rows(dbuf, d, 2, gx < 31)
    edge_rows(dbuf, d, 2, gx < 31)

    @pl.loop(0, ROWS // 2)
    def _(i):
        c = at(i * 2, 2)
        for s, v in enumerate(up(wc, d, c)):
            dg[s, :, c] = (v * slope[s, :, c]).astype(BF)

    clear(u, 1)
    for s in range(3):
        q[:, 0:256] = dot_t(u[1], dg[s])
        pairs = [(0, 0), (0, 1), (1, 1)]
        pack(
            1, s,
            [q[e * 128:e * 128 + 64, p * 128:p * 128 + 128] for e, p in pairs],
            [q[e * 128 + 64:e * 128 + 128, p * 128:p * 128 + 128] for e, p in pairs],
        )

    pair = rcopy(part.at[1 - core], core_rx, csem.at[0], csem.at[1], core_dev)
    pair.start()
    for n in range(8):
        halo(sbuf, n, s_s, s_r).wait_send()
        halo(dbuf, n, d_s, d_r).wait_send()
    pair.wait()

    def loss_tile(t):
        return jnp.logical_and(core == 0, t == 13)

    def to_owner(dst, src):
        return rcopy(psend.at[dst], plane_rx.at[src], p_s.at[dst], p_r.at[src], plane_dev(dst))

    @pl.loop(1, 17)
    def _(i):
        t = (pme + i) % 16

        @pl.when(t < TILES)
        def _():
            psend[t] = split_round(part[core, t] + core_rx[t], loss_tile(t))

            @pl.when(t != pme)
            def _():
                to_owner(t, pme).start()

    @pl.loop(0, ROWS // 2)
    def _(i):
        c = at(i * 2, 2)
        q[:, c] = down(wg, dg, c)

    @pl.loop(1, 9)
    def _(r):
        sg_ref[r - 1] = gathered(r)

    def along_z(dst, src):
        return rcopy(z_rx.at[src], z_rx.at[src], z_s.at[dst], z_r.at[src], z_dev(dst))

    def to_plane(dst, src):
        return rcopy(fin.at[core, src], fin.at[core, src], g_s.at[dst], g_r.at[src], plane_dev(dst))

    def to_core(g, t):
        return rcopy(fin.at[g, t], fin.at[g, t], f_s.at[t], f_r.at[t], core_dev)

    @pl.when(pme < TILES)
    def _():
        plane_rx[pme] = psend[pme]

        @pl.loop(1, 16)
        def _(i):
            t = (pme + i) % 16
            to_owner(pme, t).wait_recv()

        total = plane_rx[0].astype(F32)
        for t in range(1, 16):
            total += plane_rx[t].astype(F32)
        z_rx[z] = split_round(total, loss_tile(pme))

        @pl.loop(1, 8)
        def _(i):
            along_z((z + i) % 8, z).start()

        @pl.loop(1, 8)
        def _(i):
            t = (z + i) % 8
            along_z(t, t).wait_recv()

        total = z_rx[0].astype(F32)
        for t in range(1, 8):
            total += z_rx[t].astype(F32)
        fin[core, pme] = split_round(total, loss_tile(pme))
        to_core(core, pme).start()

        @pl.loop(1, 16)
        def _(i):
            to_plane((pme + i) % 16, pme).start()

    @pl.loop(1, 16)
    def _(i):
        t = (pme + 16 - i) % 16

        @pl.when(t < TILES)
        def _():
            to_plane(pme, t).wait_recv()
            to_core(core, t).start()

    @pl.loop(0, TILES)
    def _(t):
        to_core(1 - core, t).wait_recv()

    root = 1.0 / math.sqrt(262144.0)
    for g, out, full_taps, half_tap in ((0, gc_ref, (2, 0), 1), (1, gg_ref, (1, 2), 0)):
        for n in range(9):
            first = (n // 3) * 9 + (1, 2, 0)[n % 3] * 3
            full = fin[g, n].astype(F32) * root
            out[first + full_taps[0]] = full[:, 0:64]
            out[first + full_taps[1]] = full[:, 64:128]
            half = fin[g, 9 + n // 2].astype(F32) * root
            out[first + half_tap] = half[:, 0:64] if n % 2 == 0 else half[:, 64:128]
    loss = fin[0, 13].astype(F32)
    loss = loss[0:16] + loss[16:32] + loss[32:48]
    score_ref[0, 0] = jnp.sum(jnp.where(jnp.logical_and(lane((16, 128)) == 64, lax.broadcasted_iota(jnp.int32, (16, 128), 0) == 0), loss, 0.0)) * (1.0 / 262144.0)

    @pl.loop(1, 16)
    def _(i):
        t = (pme + i) % 16

        @pl.when(t < TILES)
        def _():
            to_owner(t, pme).wait_send()

    @pl.when(pme < TILES)
    def _():
        @pl.loop(1, 8)
        def _(i):
            along_z((z + i) % 8, z).wait_send()

        @pl.loop(1, 16)
        def _(i):
            to_plane((pme + i) % 16, pme).wait_send()

    @pl.loop(0, TILES)
    def _(t):
        to_core(core, t).wait_send()


def shards(sources, generator_weight, critic_kernel_weight, readout, load_weight):
    vmem = pl.BlockSpec(memory_space=pltpu.VMEM)
    smem = pl.BlockSpec(memory_space=pltpu.SMEM)
    dma = pltpu.SemaphoreType.DMA
    score, source_gradient, gen, crit = pl.pallas_call(
        kernel,
        out_shape=(
            jax.ShapeDtypeStruct((1, 1), F32),
            jax.ShapeDtypeStruct((8, 64, 128), F32),
            jax.ShapeDtypeStruct((27, 64, 64), F32),
            jax.ShapeDtypeStruct((27, 64, 64), F32),
        ),
        in_specs=[vmem, vmem, vmem, vmem, smem],
        out_specs=(smem, vmem, vmem, vmem),
        scratch_shapes=[
            pltpu.VMEM((64, 8, 128), F32),
            pltpu.VMEM((3, ROWS, 64, 128), BF),
            pltpu.VMEM((3, ROWS, 64, 128), BF),
            pltpu.VMEM((3, 256, 256), BF),
            pltpu.VMEM((3, 256, 256), BF),
            pltpu.VMEM((3, 256, 256), BF),
            pltpu.VMEM((3, 256, 256), BF),
            pltpu.VMEM((3, 256, LANES), BF),
            pltpu.VMEM((3, 256, LANES), BF),
            pltpu.VMEM((3, 256, LANES), BF),
            pltpu.VMEM((3, 256, LANES), F32),
            pltpu.VMEM((3, 256, LANES), BF),
            pltpu.VMEM((256, LANES), F32),
            pltpu.VMEM((64, 128), F32),
            pltpu.VMEM((1, 128), F32),
            pltpu.VMEM((2, TILES, 64, 128), F32),
            pltpu.VMEM((TILES, 64, 128), F32),
            pltpu.VMEM((TILES, 64, 128), BF),
            pltpu.VMEM((16, 64, 128), BF),
            pltpu.VMEM((8, 64, 128), BF),
            pltpu.VMEM((2, TILES, 64, 128), BF),
            dma((8,)), dma((8,)), dma((8,)), dma((8,)), dma((2,)),
            dma((TILES,)), dma((16,)), dma((8,)), dma((8,)),
            dma((16,)), dma((TILES,)), dma((TILES,)), dma((TILES,)),
        ],
        compiler_params=pltpu.CompilerParams(
            collective_id=0, has_side_effects=True, vmem_limit_bytes=56 * 2**20
        ),
        cost_estimate=pl.CostEstimate(flops=3 * 10**9, bytes_accessed=4 * 10**6, transcendentals=2 * 10**6),
    )(
        sources.reshape(64, 8, 128),
        generator_weight.reshape(27, 64, 64),
        critic_kernel_weight.reshape(27, 64, 64),
        readout.reshape(1, 64),
        load_weight,
    )
    return (
        score.reshape(()),
        jnp.swapaxes(source_gradient, 0, 1).reshape(1, 64, 1, 8, 128),
        gen.reshape(3, 3, 3, 64, 64),
        crit.reshape(3, 3, 3, 64, 64),
    )


def solution(mesh):
    placed = (P(None, None, "gx", "gy", None), P(), P(), P(), P("gx", "gy"))
    return jax.shard_map(
        shards,
        mesh=mesh,
        in_specs=placed,
        out_specs=(P(), P(None, None, "gx", "gy", None), P(), P()),
        check_vma=False,
    )
```

time: 566 us -> 69.6 us (0.12); the launches traced: 556 us -> 69.4 us
  waiting for transfers between devices: 257 us -> 0 us
  local copies, waits for them, and re-layouts: 99.1 us -> 4.98 us
  blocking collectives: 85.1 us -> 0 us
  Pallas kernels: 0 us -> 62 us
  matrix products: 43.2 us -> 0 us
  starting transfers between devices: 27.7 us -> 0 us
  other arithmetic: 27.2 us -> 0 us
  between operations: 16.5 us -> 2.47 us
    psum x1 -> x0, waiting for transfers between devices: 242 us -> none  [shards(): lax.psum((loss_sum, gen_grad, crit_grad), ('gx', 'gy'))]
    psum x1 -> x0, blocking collectives: 85.1 us -> none  [shards(): lax.psum((loss_sum, gen_grad, crit_grad), ('gx', 'gy'))]
    pallas_call x0 -> x1, Pallas kernels: none -> 62 us  [shards(): pl.pallas_call(kernel, out_shape=(jax.ShapeDtypeStruct((1, 1), F32), jax....]
    conv_general_dilated x12 -> x0, local copies, waits for them, and re-layouts: 36.9 us -> none  [the longest x8 36.7 us: coarsen_field(): lax.conv_general_dilated(source_field, kernel_taps, (2, 2, 2), [planar_pa...]
    ppermute x8 -> x0, starting transfers between devices: 27.7 us -> none  [passed_along(): lax.ppermute(value, axis, [(source, source + steps) for source in range(f...]
    concatenate x8 -> x0, local copies, waits for them, and re-layouts: 24.7 us -> none  [extend_halo(): jnp.concatenate([source_field, arrived] if step_dir < 0 else [arrived, so...]
    transpose x2 -> x0, matrix products: 24.6 us -> none  [the longest x1 16.7 us: critic_taps(): return jnp.transpose(taps_out, (2, 3, 4, 0, 1))]
    concatenate x9 -> x0, other arithmetic: 19.3 us -> none  [extend_halo(): jnp.concatenate([source_field, arrived] if step_dir < 0 else [arrived, so...]
  transfers between devices with their start and end apart: 9 -> 0, of which waited for: 6 -> 0; matrix products, arithmetic and copies ran while one was open for 8% -> 0% of each run, Pallas kernels for 0% -> 0%
where the time goes in v1:
time: 69.6 us; the launch traced here: 69.4 us
  Pallas kernels  62 us (89%)
  local copies, waits for them, and re-layouts  4.98 us (7%)
  between operations  2.47 us (4%)
    pallas_call x1, Pallas kernels, shards(): pl.pallas_call(kernel, out_shape=(jax.ShapeDtypeStruct((1, 1), F32), jax....  62 us
    unnamed x5, local copies, waits for them, and re-layouts  4.98 us

profile of v1, /device:TPU:1, one launch (start us, length us, event | category | flops | bytes accessed | tf_op | source)
XLA Modules:
  0.0 69.4 jit_solution(9327663016906970670)
XLA Ops:
  0.6 62.0 %shard_map.84 = (f32[1,1]{1,0:T(1,128)}, f32[8,64,128]{2,1,0:T(8,128)}, f32[27,64,64]{2,1,0:T(8,128)}, f32[27,64,64]{2,1,0:T(8,128)}) custom-call(bf16[64,8,128]{2,1,0:T(8,128)(2,1)} %bitcast.15, bf16[27,64,64]{2,1,0:T(8,128)(2,1)} %bitcast.13, bf16[27,64,64]{2,1,0:T(8,128)(2,1)} %bitcast.14, f32[1,64]{1,0:T(1,128)} %bitcast.16, s32[1,8]{1,0:T(1,128)} %lw_ref.1), custom_call_target="tpu_custom_call" | custom-call | flops 3000000000 | bytes 4000000 | tf_op jit(solution)/shard_map/pallas_call | solution.py:420
  62.6 1.8 %copy.9 = f32[1,64,1,8,128]{4,3,2,1,0:T(8,128)} copy(f32[1,64,1,8,128]{4,1,3,2,0:T(8,128)} %bitcast.12) | data formatting | bytes 524288
  65.1 0.0 copy-start
  65.1 2.3 %copy.14 = f32[3,3,3,64,64]{4,3,2,1,0:T(8,128)} copy(f32[3,3,3,64,64]{4,3,2,1,0:T(8,128)} %bitcast.11) | data formatting | bytes 884736
  67.4 0.0 copy-done
  67.4 0.9 %copy.15 = f32[3,3,3,64,64]{4,3,2,1,0:T(8,128)} copy(f32[3,3,3,64,64]{4,3,2,1,0:T(8,128)S(1)} %bitcast.10) | data formatting | bytes 884736
Async XLA Ops:
  65.1 2.3 %copy-start = (f32[27,64,64]{2,1,0:T(8,128)S(1)}, f32[27,64,64]{2,1,0:T(8,128)}, u32[]{:S(2)}) copy-start(f32[27,64,64]{2,1,0:T(8,128)} %get-tuple-element.11) | copy-start | bytes 1327108

commit v2 on v1

--- a/solution.py
+++ b/solution.py
@@ -10,7 +10,7 @@
 MESH = pl.DeviceIdType.MESH
 BF = jnp.bfloat16
 F32 = jnp.float32
-ROWS = 10
+ROWS = 9
 LANES = ROWS * 128
 TILES = 14
 TAP = {(0, 0): 1, (1, 0): 2, (1, 1): 0}
@@ -56,10 +56,10 @@
 
 
 def kernel(
-    src_ref, wg_ref, wc_ref, ro_ref, lw_ref,
-    score_ref, sg_ref, gg_ref, gc_ref,
-    stage, sbuf, dbuf, wg, wgt, wc, wct, u, d, f, slope, dg, q, ro, lossv,
-    part, core_rx, psend, plane_rx, z_rx, fin,
+    src_hbm, wg_hbm, wc_hbm, ro_hbm, lw_ref,
+    sg_ref, fin,
+    src_ref, wg_ref, wc_ref, ro_ref, lsem, half_field, stage, sbuf, dbuf, wg, wgt, wc, wct, u, d, f, slope, dg, q, ro, lossv,
+    part, core_rx, psend, plane_rx, z_rx,
     s_s, s_r, d_s, d_r, csem, p_s, p_r, z_s, z_r, g_s, g_r, f_s, f_r,
 ):
     gx, gy = lax.axis_index("gx"), lax.axis_index("gy")
@@ -82,11 +82,21 @@
             src_ref=src, dst_ref=dst, send_sem=send, recv_sem=recv, device_id=dev, device_id_type=MESH
         )
 
-    def halo(buf, n, send, recv):
+    def halo(buf, n, send, recv, half=0):
         dx, dy = SIDES[n]
-        here = pl.ds(1, 8) if dy == 0 else pl.ds(8 if dy > 0 else 1, 1)
-        there = pl.ds(1, 8) if dy == 0 else pl.ds(0 if dy > 0 else 9, 1)
-        return rcopy(buf.at[1, here], buf.at[1 - dx, there], send.at[n], recv.at[n], side_dev(SIDES[n]))
+        if dy == 0:
+            here = there = pl.ds(1 + 4 * half, 4)
+        else:
+            here, there = pl.ds(8 if dy > 0 else 1, 1), pl.ds(0 if dy > 0 else 9, 1)
+        n = n + 8 * half
+        return rcopy(buf.at[1, here], buf.at[1 - dx, there], send.at[n], recv.at[n], side_dev((dx, dy)))
+
+    loads = [
+        pltpu.make_async_copy(a, b, lsem.at[n])
+        for n, (a, b) in enumerate(((src_hbm, src_ref), (wg_hbm, wg_ref), (wc_hbm, wc_ref), (ro_hbm, ro_ref)))
+    ]
+    for load in loads:
+        load.start()
 
     barrier = pltpu.get_barrier_semaphore()
 
@@ -105,13 +115,17 @@
     def _(t):
         greet(z_dev((z + t) % 8))
 
+    loads[0].wait()
     stage[...] = src_ref[...].astype(F32)
     for r in range(8):
         sbuf[1, r + 1] = stage[:, r, :].astype(BF)
 
     pl.semaphore_wait(barrier, 8 + 1 + 15 + 7)
-    for n in range(8):
-        halo(sbuf, n, s_s, s_r).start()
+    parts = [(0, 0), (1, 0), (0, 1), (1, 1)] + [(n, 0) for n in range(2, 8)]
+    for n, half in parts:
+        halo(sbuf, n, s_s, s_r, half).start()
+    for load in loads[1:]:
+        load.wait()
 
     zero = jnp.zeros((64, 64), F32)
     for s in range(3):
@@ -150,12 +164,10 @@
     def clear(out, xs):
         nothing = jnp.zeros((128, 128), BF)
         out[xs, 0:128, at(0)] = nothing
-        out[xs, 0:128, at(9)] = nothing
         out[xs, 128:256, at(8)] = nothing
-        out[xs, 128:256, at(9)] = nothing
 
     def own_rows(buf, out, xs, keep=None):
-        @pl.loop(1, 9)
+        @pl.loop(1, 9, unroll=4)
         def _(r):
             pair = spread(buf, out, xs, r, keep)
             put_here(out, xs, r, pair)
@@ -169,8 +181,42 @@
     own_rows(sbuf, u, 1)
     clear(d, 1)
 
-    for n in range(8):
-        halo(sbuf, n, s_s, s_r).wait_recv()
+    def fire(s, v, c):
+        t = jnp.tanh(0.5 * v)
+        f[s, :, c] = (jnp.maximum(v, 0.2 * v) - 0.8 * jnp.log(1.0 + jnp.abs(t))).astype(BF)
+        slope[s, :, c] = 0.6 + 0.4 * t
+
+    def fire_low(s, v):
+        t = jnp.tanh(0.5 * v)
+        f[s, 128:256, 0:128] = (jnp.maximum(v, 0.2 * v) - 0.8 * jnp.log(1.0 + jnp.abs(t))).astype(BF)
+        slope[s, 128:256, 0:128] = 0.6 + 0.4 * t
+
+    def up_mid(weights, field, c):
+        mid = field[1, :, c]
+        return dot(weights[0], mid), dot(weights[1], mid), dot(weights[2], mid)
+
+    def up_rest(weights, field, c):
+        return dot(weights[2], field[0, :, c]), dot(weights[0], field[2, :, c])
+
+    def up_low(weights, field):
+        below, mid, above = field[0, :, 0:128], field[1, :, 0:128], field[2, :, 0:128]
+        w0, w1, w2 = (weights[k, 128:256, :] for k in range(3))
+        return dot(w2, below) + dot(w0, mid), dot(w1, mid), dot(w2, mid) + dot(w0, above)
+
+    @pl.loop(0, 3)
+    def _(j):
+        c = at(j * 2 + 1, 2)
+        low, mid, high = up_mid(wgt, u, c)
+        fire(1, mid, c)
+        slope[0, :, c] = low
+        slope[2, :, c] = high
+
+    for s in range(3):
+        f[s, 0:128, 0:128] = jnp.zeros((128, 128), BF)
+        dg[s, 0:128, 0:128] = jnp.zeros((128, 128), BF)
+
+    for n, half in parts:
+        halo(sbuf, n, s_s, s_r, half).wait_recv()
     for xs in (0, 2):
         clear(u, xs)
     edge_rows(sbuf, u, 1)
@@ -179,21 +225,20 @@
     own_rows(sbuf, u, 2, gx < 31)
     edge_rows(sbuf, u, 2, gx < 31)
 
-    def up(weights, field, c):
-        mid = field[1, :, c]
-        return (
-            dot(weights[2], field[0, :, c]) + dot(weights[0], mid),
-            dot(weights[1], mid),
-            dot(weights[2], mid) + dot(weights[0], field[2, :, c]),
-        )
-
-    @pl.loop(0, ROWS // 2)
-    def _(i):
-        c = at(i * 2, 2)
-        for s, v in enumerate(up(wgt, u, c)):
-            t = jnp.tanh(0.5 * v)
-            f[s, :, c] = (jnp.maximum(v, 0.2 * v) - 0.8 * jnp.log(1.0 + jnp.abs(t))).astype(BF)
-            slope[s, :, c] = 0.6 + 0.4 * t
+    for s, v in enumerate(up_low(wgt, u)):
+        fire_low(s, v)
+    c = at(7, 2)
+    low, mid, high = up_mid(wgt, u, c)
+    fire(1, mid, c)
+    slope[0, :, c] = low
+    slope[2, :, c] = high
+
+    @pl.loop(0, 4)
+    def _(j):
+        c = at(j * 2 + 1, 2)
+        low, high = up_rest(wgt, u, c)
+        fire(0, slope[0, :, c] + low, c)
+        fire(2, slope[2, :, c] + high, c)
 
     @pl.when(gx == 0)
     def _():
@@ -203,26 +248,25 @@
     @pl.when(gy == 0)
     def _():
         for s in range(3):
-            f[s, :, 0:128] = jnp.zeros((256, 128), BF)
-            slope[s, :, 0:128] = jnp.zeros((256, 128), F32)
+            f[s, 128:256, 0:128] = jnp.zeros((128, 128), BF)
+            slope[s, 128:256, 0:128] = jnp.zeros((128, 128), F32)
 
     def down(weights, field, c):
         return dot(weights[0], field[0, :, c]) + dot(weights[1], field[1, :, c]) + dot(weights[2], field[2, :, c])
+
+    def down_low(weights, field):
+        terms = [dot(weights[k, 128:256, 128:256], field[k, 128:256, 0:128]) for k in range(3)]
+        return terms[0] + terms[1] + terms[2]
 
     def gathered(r):
         near = q[0:64, at(r)] + q[128:192, at(r - 1)]
         far = q[64:128, at(r)] + q[192:256, at(r - 1)]
         return near + prev_z(far)
 
-    @pl.loop(0, ROWS // 2)
-    def _(i):
-        c = at(i * 2, 2)
-        q[:, c] = down(wct, f, c)
-
+    q[128:256, 0:128] = down_low(wct, f)
     lossv[...] = jnp.zeros((1, 128), F32)
 
-    @pl.loop(1, 9)
-    def _(r):
+    def judge(r):
         v = gathered(r)
         t = jnp.tanh(0.5 * v)
         act = jnp.maximum(v, 0.2 * v) - 0.8 * jnp.log(1.0 + jnp.abs(t))
@@ -233,9 +277,27 @@
         d_logit = -weight * jnp.where(logits >= 0, e, 1.0) / (1.0 + e)
         dbuf[1, r] = (d_logit * ro[...] * (0.6 + 0.4 * t)).astype(BF)
 
-    for n in range(8):
-        halo(dbuf, n, d_s, d_r).start()
+    for half in range(2):
+        @pl.loop(2 * half, 2 * half + 2)
+        def _(j):
+            c = at(j * 2 + 1, 2)
+            q[:, c] = down(wct, f, c)
+            judge(2 * j + 1)
+            judge(2 * j + 2)
+
+        for n in (0, 1):
+            halo(dbuf, n, d_s, d_r, half).start()
+        for n in (3, 5, 7) if half == 0 else (2, 4, 6):
+            halo(dbuf, n, d_s, d_r).start()
     own_rows(dbuf, d, 1)
+
+    @pl.loop(0, 3)
+    def _(j):
+        c = at(j * 2 + 1, 2)
+        low, mid, high = up_mid(wc, d, c)
+        dg[1, :, c] = (mid * slope[1, :, c]).astype(BF)
+        half_field[0, :, c] = low
+        half_field[1, :, c] = high
 
     def pack(g, s, full, halves):
         for j in range(3):
@@ -262,8 +324,8 @@
     put = lane((16, 128)) >= 64
     part[0, 13, 0:16, :] = jnp.where(put, loss, part[0, 13, 0:16, :])
 
-    for n in range(8):
-        halo(dbuf, n, d_s, d_r).wait_recv()
+    for n, half in parts:
+        halo(dbuf, n, d_s, d_r, half).wait_recv()
     for xs in (0, 2):
         clear(d, xs)
     edge_rows(dbuf, d, 1)
@@ -272,11 +334,20 @@
     own_rows(dbuf, d, 2, gx < 31)
     edge_rows(dbuf, d, 2, gx < 31)
 
-    @pl.loop(0, ROWS // 2)
-    def _(i):
-        c = at(i * 2, 2)
-        for s, v in enumerate(up(wc, d, c)):
-            dg[s, :, c] = (v * slope[s, :, c]).astype(BF)
+    for s, v in enumerate(up_low(wc, d)):
+        dg[s, 128:256, 0:128] = (v * slope[s, 128:256, 0:128]).astype(BF)
+    c = at(7, 2)
+    low, mid, high = up_mid(wc, d, c)
+    dg[1, :, c] = (mid * slope[1, :, c]).astype(BF)
+    half_field[0, :, c] = low
+    half_field[1, :, c] = high
+
+    @pl.loop(0, 4)
+    def _(j):
+        c = at(j * 2 + 1, 2)
+        low, high = up_rest(wc, d, c)
+        dg[0, :, c] = ((half_field[0, :, c] + low) * slope[0, :, c]).astype(BF)
+        dg[2, :, c] = ((half_field[1, :, c] + high) * slope[2, :, c]).astype(BF)
 
     clear(u, 1)
     for s in range(3):
@@ -290,9 +361,9 @@
 
     pair = rcopy(part.at[1 - core], core_rx, csem.at[0], csem.at[1], core_dev)
     pair.start()
-    for n in range(8):
-        halo(sbuf, n, s_s, s_r).wait_send()
-        halo(dbuf, n, d_s, d_r).wait_send()
+    for n, half in parts:
+        halo(sbuf, n, s_s, s_r, half).wait_send()
+        halo(dbuf, n, d_s, d_r, half).wait_send()
     pair.wait()
 
     def loss_tile(t):
@@ -313,14 +384,14 @@
             def _():
                 to_owner(t, pme).start()
 
-    @pl.loop(0, ROWS // 2)
-    def _(i):
-        c = at(i * 2, 2)
+    q[128:256, 0:128] = down_low(wg, dg)
+
+    @pl.loop(0, 4)
+    def _(j):
+        c = at(j * 2 + 1, 2)
         q[:, c] = down(wg, dg, c)
-
-    @pl.loop(1, 9)
-    def _(r):
-        sg_ref[r - 1] = gathered(r)
+        sg_ref[2 * j] = gathered(2 * j + 1)
+        sg_ref[2 * j + 1] = gathered(2 * j + 2)
 
     def along_z(dst, src):
         return rcopy(z_rx.at[src], z_rx.at[src], z_s.at[dst], z_r.at[src], z_dev(dst))
@@ -377,6 +448,32 @@
     def _(t):
         to_core(1 - core, t).wait_recv()
 
+    @pl.loop(1, 16)
+    def _(i):
+        t = (pme + i) % 16
+
+        @pl.when(t < TILES)
+        def _():
+            to_owner(t, pme).wait_send()
+
+    @pl.when(pme < TILES)
+    def _():
+        @pl.loop(1, 8)
+        def _(i):
+            along_z((z + i) % 8, z).wait_send()
+
+        @pl.loop(1, 16)
+        def _(i):
+            to_plane((pme + i) % 16, pme).wait_send()
+
+    @pl.loop(0, TILES)
+    def _(t):
+        to_core(core, t).wait_send()
+
+
+def unpack(fin, sg_ref, score_ref, sgo_ref, gg_ref, gc_ref):
+    for r in range(8):
+        sgo_ref[:, r, :] = sg_ref[r]
     root = 1.0 / math.sqrt(262144.0)
     for g, out, full_taps, half_tap in ((0, gc_ref, (2, 0), 1), (1, gg_ref, (1, 2), 0)):
         for n in range(9):
@@ -390,47 +487,30 @@
     loss = loss[0:16] + loss[16:32] + loss[32:48]
     score_ref[0, 0] = jnp.sum(jnp.where(jnp.logical_and(lane((16, 128)) == 64, lax.broadcasted_iota(jnp.int32, (16, 128), 0) == 0), loss, 0.0)) * (1.0 / 262144.0)
 
-    @pl.loop(1, 16)
-    def _(i):
-        t = (pme + i) % 16
-
-        @pl.when(t < TILES)
-        def _():
-            to_owner(t, pme).wait_send()
-
-    @pl.when(pme < TILES)
-    def _():
-        @pl.loop(1, 8)
-        def _(i):
-            along_z((z + i) % 8, z).wait_send()
-
-        @pl.loop(1, 16)
-        def _(i):
-            to_plane((pme + i) % 16, pme).wait_send()
-
-    @pl.loop(0, TILES)
-    def _(t):
-        to_core(core, t).wait_send()
-
 
 def shards(sources, generator_weight, critic_kernel_weight, readout, load_weight):
     vmem = pl.BlockSpec(memory_space=pltpu.VMEM)
     smem = pl.BlockSpec(memory_space=pltpu.SMEM)
     dma = pltpu.SemaphoreType.DMA
-    score, source_gradient, gen, crit = pl.pallas_call(
+    hbm = pl.BlockSpec(memory_space=pl.ANY)
+    source_gradient, taps = pl.pallas_call(
         kernel,
         out_shape=(
-            jax.ShapeDtypeStruct((1, 1), F32),
             jax.ShapeDtypeStruct((8, 64, 128), F32),
-            jax.ShapeDtypeStruct((27, 64, 64), F32),
-            jax.ShapeDtypeStruct((27, 64, 64), F32),
+            jax.ShapeDtypeStruct((2, TILES, 64, 128), BF),
         ),
-        in_specs=[vmem, vmem, vmem, vmem, smem],
-        out_specs=(smem, vmem, vmem, vmem),
+        in_specs=[hbm, hbm, hbm, hbm, smem],
+        out_specs=(vmem, vmem),
         scratch_shapes=[
+            pltpu.VMEM((64, 8, 128), BF),
+            pltpu.VMEM((27, 64, 64), BF),
+            pltpu.VMEM((27, 64, 64), BF),
+            pltpu.VMEM((1, 64), F32),
+            dma((4,)),
+            pltpu.VMEM((2, 256, LANES), F32),
             pltpu.VMEM((64, 8, 128), F32),
-            pltpu.VMEM((3, ROWS, 64, 128), BF),
-            pltpu.VMEM((3, ROWS, 64, 128), BF),
+            pltpu.VMEM((3, 10, 64, 128), BF),
+            pltpu.VMEM((3, 10, 64, 128), BF),
             pltpu.VMEM((3, 256, 256), BF),
             pltpu.VMEM((3, 256, 256), BF),
             pltpu.VMEM((3, 256, 256), BF),
@@ -448,8 +528,7 @@
             pltpu.VMEM((TILES, 64, 128), BF),
             pltpu.VMEM((16, 64, 128), BF),
             pltpu.VMEM((8, 64, 128), BF),
-            pltpu.VMEM((2, TILES, 64, 128), BF),
-            dma((8,)), dma((8,)), dma((8,)), dma((8,)), dma((2,)),
+            dma((16,)), dma((16,)), dma((16,)), dma((16,)), dma((2,)),
             dma((TILES,)), dma((16,)), dma((8,)), dma((8,)),
             dma((16,)), dma((TILES,)), dma((TILES,)), dma((TILES,)),
         ],
@@ -464,9 +543,21 @@
         readout.reshape(1, 64),
         load_weight,
     )
+    score, source_gradient, gen, crit = pl.pallas_call(
+        unpack,
+        out_shape=(
+            jax.ShapeDtypeStruct((1, 1), F32),
+            jax.ShapeDtypeStruct((64, 8, 128), F32),
+            jax.ShapeDtypeStruct((27, 64, 64), F32),
+            jax.ShapeDtypeStruct((27, 64, 64), F32),
+        ),
+        in_specs=[vmem, vmem],
+        out_specs=(smem, vmem, vmem, vmem),
+        compiler_params=pltpu.CompilerParams(vmem_limit_bytes=16 * 2**20),
+    )(taps, source_gradient)
     return (
         score.reshape(()),
-        jnp.swapaxes(source_gradient, 0, 1).reshape(1, 64, 1, 8, 128),
+        source_gradient.reshape(1, 64, 1, 8, 128),
         gen.reshape(3, 3, 3, 64, 64),
         crit.reshape(3, 3, 3, 64, 64),
     )

time: 69.6 us -> 61.4 us (0.88)
  Pallas kernels: 62 us -> 58.6 us
  local copies, waits for them, and re-layouts: 4.98 us -> 1.96 us
  between operations: 2.47 us -> 0.65 us
    pallas_call x1 -> x2, Pallas kernels: 62 us -> 58.6 us  [the longest x1 57 us: shards(): pl.pallas_call(kernel, out_shape=(jax.ShapeDtypeStruct((8, 64, 128), F32)...]
    unnamed x5 -> x4, local copies, waits for them, and re-layouts: 4.98 us -> 1.96 us
where the time goes in v2:
time: 61.4 us; the launch traced here: 61.2 us
  Pallas kernels  58.6 us (95%)
  local copies, waits for them, and re-layouts  1.96 us (3%)
  between operations  0.65 us (1%)
    pallas_call x1, Pallas kernels, shards(): pl.pallas_call(kernel, out_shape=(jax.ShapeDtypeStruct((8, 64, 128), F32)...  57 us
    unnamed x4, local copies, waits for them, and re-layouts  1.96 us
    pallas_call x1, Pallas kernels, shards(): pl.pallas_call(unpack, out_shape=(jax.ShapeDtypeStruct((1, 1), F32), jax....  1.63 us

profile of v2, /device:TPU:1, one launch (start us, length us, event | category | flops | bytes accessed | tf_op | source)
XLA Modules:
  0.0 61.2 jit_solution(3941247045151941739)
XLA Ops:
  0.6 57.0 %shard_map.84 = (f32[8,64,128]{2,1,0:T(8,128)}, bf16[2,14,64,128]{3,2,1,0:T(8,128)(2,1)}) custom-call(bf16[64,8,128]{2,1,0:T(8,128)(2,1)} %bitcast.15, bf16[27,64,64]{2,1,0:T(8,128)(2,1)} %bitcast.12, bf16[27,64,64]{2,1,0:T(8,128)(2,1)} %bitcast.13, f32[1,64]{1,0:T(1,128)} %bitcast.16, s32[1,8]{1,0:T(1,128)} %lw_ref.1), custom_call_target="tpu_custom_call" | custom-call | flops 3000000000 | bytes 4000000 | tf_op jit(solution)/shard_map/pallas_call | solution.py:496
  57.6 0.0 copy-start
  57.7 1.0 %copy-done = bf16[2,14,64,128]{3,2,1,0:T(8,128)(2,1)S(1)} copy-done((bf16[2,14,64,128]{3,2,1,0:T(8,128)(2,1)S(1)}, bf16[2,14,64,128]{3,2,1,0:T(8,128)(2,1)}, u32[]{:S(2)}) %copy-start) | copy-done | bytes 458776
  58.7 0.0 copy-start.1
  58.7 0.9 %copy-done.1 = f32[8,64,128]{2,1,0:T(8,128)S(1)} copy-done((f32[8,64,128]{2,1,0:T(8,128)S(1)}, f32[8,64,128]{2,1,0:T(8,128)}, u32[]{:S(2)}) %copy-start.1) | copy-done | bytes 262168
  59.6 1.6 %shard_map.85 = (f32[1,1]{1,0:T(1,128)}, f32[64,8,128]{2,1,0:T(8,128)}, f32[27,64,64]{2,1,0:T(8,128)}, f32[27,64,64]{2,1,0:T(8,128)}) custom-call(bf16[2,14,64,128]{3,2,1,0:T(8,128)(2,1)S(1)} %copy-done, f32[8,64,128]{2,1,0:T(8,128)S(1)} %copy-done.1), custom_call_target="tpu_custom_call" | custom-call | tf_op jit(solution)/shard_map/pallas_call | solution.py:546
Async XLA Ops:
  57.6 1.0 %copy-start = (bf16[2,14,64,128]{3,2,1,0:T(8,128)(2,1)S(1)}, bf16[2,14,64,128]{3,2,1,0:T(8,128)(2,1)}, u32[]{:S(2)}) copy-start(bf16[2,14,64,128]{3,2,1,0:T(8,128)(2,1)} %get-tuple-element.10.fin) | copy-start | bytes 1376260
  58.7 0.9 %copy-start.1 = (f32[8,64,128]{2,1,0:T(8,128)S(1)}, f32[8,64,128]{2,1,0:T(8,128)}, u32[]{:S(2)}) copy-start(f32[8,64,128]{2,1,0:T(8,128)} %get-tuple-element.11.sg_ref) | copy-start | bytes 786436

commit v3 on v2

--- a/solution.py
+++ b/solution.py
@@ -43,7 +43,7 @@
     return pl.ds(pl.multiple_of(row * 128, 128), count * 128)
 
 
-def split_round(value, holds_loss):
+def split_round(value):
     plain = value.astype(BF)
     loss = value[0:16] + value[16:32] + value[32:48]
     high = loss.astype(BF)
@@ -51,8 +51,7 @@
     middle = rest.astype(BF)
     low = (rest - middle.astype(F32)).astype(BF)
     parts = jnp.concatenate([high, middle, low, jnp.zeros_like(high)], 0).astype(F32)
-    use = jnp.logical_and(lane(value.shape) >= 64, holds_loss)
-    return jnp.where(use, parts, plain.astype(F32)).astype(BF)
+    return jnp.where(lane(value.shape) >= 64, parts, plain.astype(F32)).astype(BF)
 
 
 def kernel(
@@ -60,7 +59,7 @@
     sg_ref, fin,
     src_ref, wg_ref, wc_ref, ro_ref, lsem, half_field, stage, sbuf, dbuf, wg, wgt, wc, wct, u, d, f, slope, dg, q, ro, lossv,
     part, core_rx, psend, plane_rx, z_rx,
-    s_s, s_r, d_s, d_r, csem, p_s, p_r, z_s, z_r, g_s, g_r, f_s, f_r,
+    s_s, s_r, d_s, d_r, c_s, c_r, p_s, p_r, z_s, z_r, g_s, g_r, f_s, f_r,
 ):
     gx, gy = lax.axis_index("gx"), lax.axis_index("gy")
     z, y, x, core = gx // 4, gx % 4, gy // 2, gy % 2
@@ -121,7 +120,7 @@
         sbuf[1, r + 1] = stage[:, r, :].astype(BF)
 
     pl.semaphore_wait(barrier, 8 + 1 + 15 + 7)
-    parts = [(0, 0), (1, 0), (0, 1), (1, 1)] + [(n, 0) for n in range(2, 8)]
+    parts = [(n, 0) for n in (4, 5, 6, 7, 2, 3)] + [(0, 0), (1, 0), (0, 1), (1, 1)]
     for n, half in parts:
         halo(sbuf, n, s_s, s_r, half).start()
     for load in loads[1:]:
@@ -166,20 +165,32 @@
         out[xs, 0:128, at(0)] = nothing
         out[xs, 128:256, at(8)] = nothing
 
-    def own_rows(buf, out, xs, keep=None):
-        @pl.loop(1, 9, unroll=4)
+    def own_rows(buf, out, xs, keep=None, first=1, last=8):
+        @pl.loop(first, last + 1, unroll=4)
         def _(r):
             pair = spread(buf, out, xs, r, keep)
             put_here(out, xs, r, pair)
             put_below(out, xs, r, pair)
 
+    def arrive(buf, out, send, recv):
+        for half in range(2):
+            for n, xs, keep in ((0, 0, None), (1, 2, gx < 31)):
+                halo(buf, n, send, recv, half).wait_recv()
+                own_rows(buf, out, xs, keep, 1 + 4 * half, 4 + 4 * half)
+        for n in range(2, 8):
+            halo(buf, n, send, recv).wait_recv()
+        edge_rows(buf, out, 1)
+        edge_rows(buf, out, 0)
+        edge_rows(buf, out, 2, gx < 31)
+
     def edge_rows(buf, out, xs, keep=True):
         put_here(out, xs, 0, spread(buf, out, xs, 0, keep))
         put_below(out, xs, 9, spread(buf, out, xs, 9, jnp.logical_and(keep, gy < 7)))
 
-    clear(u, 1)
+    for xs in range(3):
+        clear(u, xs)
+        clear(d, xs)
     own_rows(sbuf, u, 1)
-    clear(d, 1)
 
     def fire(s, v, c):
         t = jnp.tanh(0.5 * v)
@@ -215,15 +226,7 @@
         f[s, 0:128, 0:128] = jnp.zeros((128, 128), BF)
         dg[s, 0:128, 0:128] = jnp.zeros((128, 128), BF)
 
-    for n, half in parts:
-        halo(sbuf, n, s_s, s_r, half).wait_recv()
-    for xs in (0, 2):
-        clear(u, xs)
-    edge_rows(sbuf, u, 1)
-    own_rows(sbuf, u, 0)
-    edge_rows(sbuf, u, 0)
-    own_rows(sbuf, u, 2, gx < 31)
-    edge_rows(sbuf, u, 2, gx < 31)
+    arrive(sbuf, u, s_s, s_r)
 
     for s, v in enumerate(up_low(wgt, u)):
         fire_low(s, v)
@@ -285,10 +288,10 @@
             judge(2 * j + 1)
             judge(2 * j + 2)
 
+        for n in (5, 7, 3) if half == 0 else (4, 6, 2):
+            halo(dbuf, n, d_s, d_r).start()
         for n in (0, 1):
             halo(dbuf, n, d_s, d_r, half).start()
-        for n in (3, 5, 7) if half == 0 else (2, 4, 6):
-            halo(dbuf, n, d_s, d_r).start()
     own_rows(dbuf, d, 1)
 
     @pl.loop(0, 3)
@@ -298,6 +301,46 @@
         dg[1, :, c] = (mid * slope[1, :, c]).astype(BF)
         half_field[0, :, c] = low
         half_field[1, :, c] = high
+
+    def pair(g, k):
+        lo, count = ((0, 3), (3, 3), (6, 3), (9, 5))[k]
+        here = pl.ds(lo, count)
+        return rcopy(part.at[g, here], core_rx.at[here], c_s.at[k], c_r.at[k], core_dev)
+
+    def give(g, ks):
+        @pl.when(core == 1 - g)
+        def _():
+            for k in ks:
+                pair(g, k).start()
+
+    def loss_tile(t):
+        return jnp.logical_and(core == 0, t == 13)
+
+    def to_owner(dst, src):
+        return rcopy(psend.at[dst], plane_rx.at[src], p_s.at[dst], p_r.at[src], plane_dev(dst))
+
+    def begin_sum(g):
+        @pl.when(core == g)
+        def _():
+            for k in range(4):
+                pair(g, k).wait_recv()
+
+            @pl.loop(1, 17)
+            def _(i):
+                t = (pme + i) % 16
+
+                @pl.when(t < TILES)
+                def _():
+                    total = part[g, t] + core_rx[t]
+                    psend[t] = total.astype(BF)
+                    if g == 0:
+                        @pl.when(t == 13)
+                        def _():
+                            psend[t] = split_round(total)
+
+                    @pl.when(t != pme)
+                    def _():
+                        to_owner(t, pme).start()
 
     def pack(g, s, full, halves):
         for j in range(3):
@@ -320,19 +363,14 @@
             [q[(p * 2 + 1) * 64:(p * 2 + 2) * 64, e * 128:e * 128 + 128] for p, e in pairs],
             [q[p * 128:p * 128 + 64, e * 128:e * 128 + 128] for p, e in pairs],
         )
+        give(0, [s])
     loss = jnp.broadcast_to(jnp.sum(lossv[...], 1, keepdims=True), (16, 128))
     put = lane((16, 128)) >= 64
     part[0, 13, 0:16, :] = jnp.where(put, loss, part[0, 13, 0:16, :])
-
-    for n, half in parts:
-        halo(dbuf, n, d_s, d_r, half).wait_recv()
-    for xs in (0, 2):
-        clear(d, xs)
-    edge_rows(dbuf, d, 1)
-    own_rows(dbuf, d, 0)
-    edge_rows(dbuf, d, 0)
-    own_rows(dbuf, d, 2, gx < 31)
-    edge_rows(dbuf, d, 2, gx < 31)
+    give(0, [3])
+
+    arrive(dbuf, d, d_s, d_r)
+    begin_sum(0)
 
     for s, v in enumerate(up_low(wc, d)):
         dg[s, 128:256, 0:128] = (v * slope[s, 128:256, 0:128]).astype(BF)
@@ -358,31 +396,14 @@
             [q[e * 128:e * 128 + 64, p * 128:p * 128 + 128] for e, p in pairs],
             [q[e * 128 + 64:e * 128 + 128, p * 128:p * 128 + 128] for e, p in pairs],
         )
-
-    pair = rcopy(part.at[1 - core], core_rx, csem.at[0], csem.at[1], core_dev)
-    pair.start()
+        give(1, [s, 3] if s == 2 else [s])
+
+    begin_sum(1)
     for n, half in parts:
         halo(sbuf, n, s_s, s_r, half).wait_send()
         halo(dbuf, n, d_s, d_r, half).wait_send()
-    pair.wait()
-
-    def loss_tile(t):
-        return jnp.logical_and(core == 0, t == 13)
-
-    def to_owner(dst, src):
-        return rcopy(psend.at[dst], plane_rx.at[src], p_s.at[dst], p_r.at[src], plane_dev(dst))
-
-    @pl.loop(1, 17)
-    def _(i):
-        t = (pme + i) % 16
-
-        @pl.when(t < TILES)
-        def _():
-            psend[t] = split_round(part[core, t] + core_rx[t], loss_tile(t))
-
-            @pl.when(t != pme)
-            def _():
-                to_owner(t, pme).start()
+    for k in range(4):
+        pair(1 - core, k).wait_send()
 
     q[128:256, 0:128] = down_low(wg, dg)
 
@@ -414,7 +435,11 @@
         total = plane_rx[0].astype(F32)
         for t in range(1, 16):
             total += plane_rx[t].astype(F32)
-        z_rx[z] = split_round(total, loss_tile(pme))
+        z_rx[z] = total.astype(BF)
+
+        @pl.when(loss_tile(pme))
+        def _():
+            z_rx[z] = split_round(total)
 
         @pl.loop(1, 8)
         def _(i):
@@ -428,12 +453,18 @@
         total = z_rx[0].astype(F32)
         for t in range(1, 8):
             total += z_rx[t].astype(F32)
-        fin[core, pme] = split_round(total, loss_tile(pme))
-        to_core(core, pme).start()
+        fin[core, pme] = total.astype(BF)
+
+        @pl.when(loss_tile(pme))
+        def _():
+            fin[core, pme] = split_round(total)
+
 
         @pl.loop(1, 16)
         def _(i):
             to_plane((pme + i) % 16, pme).start()
+
+        to_core(core, pme).start()
 
     @pl.loop(1, 16)
     def _(i):
@@ -471,21 +502,34 @@
         to_core(core, t).wait_send()
 
 
-def unpack(fin, sg_ref, score_ref, sgo_ref, gg_ref, gc_ref):
-    for r in range(8):
-        sgo_ref[:, r, :] = sg_ref[r]
+def unpack(fin, sg_ref, score_ref, sg_out, gg_out, gc_out, sg_held, gg_held, gc_held, sem):
+    copies = []
+
+    def send(held, out):
+        copies.append(pltpu.make_async_copy(held, out, sem.at[len(copies)]))
+        copies[-1].start()
+
     root = 1.0 / math.sqrt(262144.0)
-    for g, out, full_taps, half_tap in ((0, gc_ref, (2, 0), 1), (1, gg_ref, (1, 2), 0)):
+    for g, held, out, full_taps, half_tap in ((0, gc_held, gc_out, (2, 0), 1), (1, gg_held, gg_out, (1, 2), 0)):
         for n in range(9):
             first = (n // 3) * 9 + (1, 2, 0)[n % 3] * 3
             full = fin[g, n].astype(F32) * root
-            out[first + full_taps[0]] = full[:, 0:64]
-            out[first + full_taps[1]] = full[:, 64:128]
+            held[first + full_taps[0]] = full[:, 0:64]
+            held[first + full_taps[1]] = full[:, 64:128]
             half = fin[g, 9 + n // 2].astype(F32) * root
-            out[first + half_tap] = half[:, 0:64] if n % 2 == 0 else half[:, 64:128]
+            held[first + half_tap] = half[:, 0:64] if n % 2 == 0 else half[:, 64:128]
+            if n % 3 == 2:
+                here = pl.ds((n // 3) * 9, 9)
+                send(held.at[here], out.at[here])
+    for r in range(8):
+        sg_held[:, r, :] = sg_ref[r]
+    send(sg_held, sg_out)
     loss = fin[0, 13].astype(F32)
     loss = loss[0:16] + loss[16:32] + loss[32:48]
-    score_ref[0, 0] = jnp.sum(jnp.where(jnp.logical_and(lane((16, 128)) == 64, lax.broadcasted_iota(jnp.int32, (16, 128), 0) == 0), loss, 0.0)) * (1.0 / 262144.0)
+    first = jnp.logical_and(lane((16, 128)) == 64, lax.broadcasted_iota(jnp.int32, (16, 128), 0) == 0)
+    score_ref[0, 0] = jnp.sum(jnp.where(first, loss, 0.0)) * (1.0 / 262144.0)
+    for copy in copies:
+        copy.wait()
 
 
 def shards(sources, generator_weight, critic_kernel_weight, readout, load_weight):
@@ -528,7 +572,7 @@
             pltpu.VMEM((TILES, 64, 128), BF),
             pltpu.VMEM((16, 64, 128), BF),
             pltpu.VMEM((8, 64, 128), BF),
-            dma((16,)), dma((16,)), dma((16,)), dma((16,)), dma((2,)),
+            dma((16,)), dma((16,)), dma((16,)), dma((16,)), dma((4,)), dma((4,)),
             dma((TILES,)), dma((16,)), dma((8,)), dma((8,)),
             dma((16,)), dma((TILES,)), dma((TILES,)), dma((TILES,)),
         ],
@@ -552,7 +596,13 @@
             jax.ShapeDtypeStruct((27, 64, 64), F32),
         ),
         in_specs=[vmem, vmem],
-        out_specs=(smem, vmem, vmem, vmem),
+        out_specs=(smem, hbm, hbm, hbm),
+        scratch_shapes=[
+            pltpu.VMEM((64, 8, 128), F32),
+            pltpu.VMEM((27, 64, 64), F32),
+            pltpu.VMEM((27, 64, 64), F32),
+            dma((7,)),
+        ],
         compiler_params=pltpu.CompilerParams(vmem_limit_bytes=16 * 2**20),
     )(taps, source_gradient)
     return (

time: 61.4 us -> 56.3 us (0.917)
  Pallas kernels: 58.6 us -> 53.5 us
    pallas_call x1, Pallas kernels: 57 us -> 51.5 us  [shards(): pl.pallas_call(kernel, out_shape=(jax.ShapeDtypeStruct((8, 64, 128), F32)...]
where the time goes in v3:
time: 56.3 us; the launch traced here: 56.1 us
  Pallas kernels  53.5 us (95%)
  local copies, waits for them, and re-layouts  1.96 us (3%)
  between operations  0.65 us (1%)
    pallas_call x1, Pallas kernels, shards(): pl.pallas_call(kernel, out_shape=(jax.ShapeDtypeStruct((8, 64, 128), F32)...  51.5 us
    pallas_call x1, Pallas kernels, shards(): pl.pallas_call(unpack, out_shape=(jax.ShapeDtypeStruct((1, 1), F32), jax....  1.96 us
    unnamed x4, local copies, waits for them, and re-layouts  1.96 us

profile of v3, /device:TPU:1, one launch (start us, length us, event | category | flops | bytes accessed | tf_op | source)
XLA Modules:
  0.0 56.1 jit_solution(11407688810886437434)
XLA Ops:
  0.6 51.5 %shard_map.84 = (f32[8,64,128]{2,1,0:T(8,128)}, bf16[2,14,64,128]{3,2,1,0:T(8,128)(2,1)}) custom-call(bf16[64,8,128]{2,1,0:T(8,128)(2,1)} %bitcast.15, bf16[27,64,64]{2,1,0:T(8,128)(2,1)} %bitcast.12, bf16[27,64,64]{2,1,0:T(8,128)(2,1)} %bitcast.13, f32[1,64]{1,0:T(1,128)} %bitcast.16, s32[1,8]{1,0:T(1,128)} %lw_ref.1), custom_call_target="tpu_custom_call" | custom-call | flops 3000000000 | bytes 4000000 | tf_op jit(solution)/shard_map/pallas_call | solution.py:540
  52.2 0.0 copy-start
  52.2 1.0 %copy-done = bf16[2,14,64,128]{3,2,1,0:T(8,128)(2,1)S(1)} copy-done((bf16[2,14,64,128]{3,2,1,0:T(8,128)(2,1)S(1)}, bf16[2,14,64,128]{3,2,1,0:T(8,128)(2,1)}, u32[]{:S(2)}) %copy-start) | copy-done | bytes 458776
  53.2 0.0 copy-start.1
  53.2 0.9 %copy-done.1 = f32[8,64,128]{2,1,0:T(8,128)S(1)} copy-done((f32[8,64,128]{2,1,0:T(8,128)S(1)}, f32[8,64,128]{2,1,0:T(8,128)}, u32[]{:S(2)}) %copy-start.1) | copy-done | bytes 262168
  54.2 2.0 %shard_map.85 = (f32[1,1]{1,0:T(1,128)}, f32[64,8,128]{2,1,0:T(8,128)}, f32[27,64,64]{2,1,0:T(8,128)}, f32[27,64,64]{2,1,0:T(8,128)}) custom-call(bf16[2,14,64,128]{3,2,1,0:T(8,128)(2,1)S(1)} %copy-done, f32[8,64,128]{2,1,0:T(8,128)S(1)} %copy-done.1), custom_call_target="tpu_custom_call" | custom-call | tf_op jit(solution)/shard_map/pallas_call | solution.py:590
Async XLA Ops:
  52.2 1.0 %copy-start = (bf16[2,14,64,128]{3,2,1,0:T(8,128)(2,1)S(1)}, bf16[2,14,64,128]{3,2,1,0:T(8,128)(2,1)}, u32[]{:S(2)}) copy-start(bf16[2,14,64,128]{3,2,1,0:T(8,128)(2,1)} %get-tuple-element.10.fin) | copy-start | bytes 1376260
  53.2 0.9 %copy-start.1 = (f32[8,64,128]{2,1,0:T(8,128)S(1)}, f32[8,64,128]{2,1,0:T(8,128)}, u32[]{:S(2)}) copy-start(f32[8,64,128]{2,1,0:T(8,128)} %get-tuple-element.11.sg_ref) | copy-start | bytes 786436

commit v4 on v3

--- a/solution.py
+++ b/solution.py
@@ -81,10 +81,11 @@
             src_ref=src, dst_ref=dst, send_sem=send, recv_sem=recv, device_id=dev, device_id_type=MESH
         )
 
-    def halo(buf, n, send, recv, half=0):
+    def halo(buf, n, send, recv, half=0, pieces=2):
         dx, dy = SIDES[n]
         if dy == 0:
-            here = there = pl.ds(1 + 4 * half, 4)
+            count = 8 // pieces
+            here = there = pl.ds(1 + count * half, count)
         else:
             here, there = pl.ds(8 if dy > 0 else 1, 1), pl.ds(0 if dy > 0 else 9, 1)
         n = n + 8 * half
@@ -120,7 +121,8 @@
         sbuf[1, r + 1] = stage[:, r, :].astype(BF)
 
     pl.semaphore_wait(barrier, 8 + 1 + 15 + 7)
-    parts = [(n, 0) for n in (4, 5, 6, 7, 2, 3)] + [(0, 0), (1, 0), (0, 1), (1, 1)]
+    parts = [(n, 0) for n in (4, 5, 6, 7, 2, 3)] + [(n, h) for h in range(2) for n in (0, 1)]
+    quarters = parts[:6] + [(n, h) for h in range(4) for n in (0, 1)]
     for n, half in parts:
         halo(sbuf, n, s_s, s_r, half).start()
     for load in loads[1:]:
@@ -166,17 +168,18 @@
         out[xs, 128:256, at(8)] = nothing
 
     def own_rows(buf, out, xs, keep=None, first=1, last=8):
-        @pl.loop(first, last + 1, unroll=4)
+        @pl.loop(first, last + 1, unroll=min(4, last + 1 - first))
         def _(r):
             pair = spread(buf, out, xs, r, keep)
             put_here(out, xs, r, pair)
             put_below(out, xs, r, pair)
 
-    def arrive(buf, out, send, recv):
-        for half in range(2):
+    def arrive(buf, out, send, recv, pieces):
+        count = 8 // pieces
+        for half in range(pieces):
             for n, xs, keep in ((0, 0, None), (1, 2, gx < 31)):
-                halo(buf, n, send, recv, half).wait_recv()
-                own_rows(buf, out, xs, keep, 1 + 4 * half, 4 + 4 * half)
+                halo(buf, n, send, recv, half, pieces).wait_recv()
+                own_rows(buf, out, xs, keep, 1 + count * half, count + count * half)
         for n in range(2, 8):
             halo(buf, n, send, recv).wait_recv()
         edge_rows(buf, out, 1)
@@ -226,7 +229,7 @@
         f[s, 0:128, 0:128] = jnp.zeros((128, 128), BF)
         dg[s, 0:128, 0:128] = jnp.zeros((128, 128), BF)
 
-    arrive(sbuf, u, s_s, s_r)
+    arrive(sbuf, u, s_s, s_r, 2)
 
     for s, v in enumerate(up_low(wgt, u)):
         fire_low(s, v)
@@ -267,31 +270,32 @@
         return near + prev_z(far)
 
     q[128:256, 0:128] = down_low(wct, f)
-    lossv[...] = jnp.zeros((1, 128), F32)
+    lossv[...] = jnp.zeros((1, 256), F32)
 
     def judge(r):
-        v = gathered(r)
+        near = q[0:64, at(r, 2)] + q[128:192, at(r - 1, 2)]
+        far = q[64:128, at(r, 2)] + q[192:256, at(r - 1, 2)]
+        v = near + jnp.where(lane((64, 256)) % 128 > 0, pltpu.roll(far, 1, 1), 0.0)
         t = jnp.tanh(0.5 * v)
         act = jnp.maximum(v, 0.2 * v) - 0.8 * jnp.log(1.0 + jnp.abs(t))
-        logits = jnp.sum(act * ro[...], 0, keepdims=True)
-        weight = lw_ref[0, r - 1].astype(F32)
+        read = jnp.concatenate([ro[...], ro[...]], 1)
+        logits = jnp.sum(act * read, 0, keepdims=True)
+        weight = jnp.where(lane((1, 256)) < 128, lw_ref[0, r - 1].astype(F32), lw_ref[0, r].astype(F32))
         e = jnp.exp(-jnp.abs(logits))
         lossv[...] += weight * (jnp.maximum(-logits, 0.0) + jnp.log1p(e))
         d_logit = -weight * jnp.where(logits >= 0, e, 1.0) / (1.0 + e)
-        dbuf[1, r] = (d_logit * ro[...] * (0.6 + 0.4 * t)).astype(BF)
-
-    for half in range(2):
-        @pl.loop(2 * half, 2 * half + 2)
-        def _(j):
-            c = at(j * 2 + 1, 2)
-            q[:, c] = down(wct, f, c)
-            judge(2 * j + 1)
-            judge(2 * j + 2)
-
-        for n in (5, 7, 3) if half == 0 else (4, 6, 2):
+        rows = (d_logit * read * (0.6 + 0.4 * t)).astype(BF)
+        dbuf[1, r] = rows[:, 0:128]
+        dbuf[1, r + 1] = rows[:, 128:256]
+
+    for j in range(4):
+        c = at(j * 2 + 1, 2)
+        q[:, c] = down(wct, f, c)
+        judge(2 * j + 1)
+        for n in {0: (5, 7, 3), 3: (4, 6, 2)}.get(j, ()):
             halo(dbuf, n, d_s, d_r).start()
         for n in (0, 1):
-            halo(dbuf, n, d_s, d_r, half).start()
+            halo(dbuf, n, d_s, d_r, j, 4).start()
     own_rows(dbuf, d, 1)
 
     @pl.loop(0, 3)
@@ -369,7 +373,7 @@
     part[0, 13, 0:16, :] = jnp.where(put, loss, part[0, 13, 0:16, :])
     give(0, [3])
 
-    arrive(dbuf, d, d_s, d_r)
+    arrive(dbuf, d, d_s, d_r, 4)
     begin_sum(0)
 
     for s, v in enumerate(up_low(wc, d)):
@@ -401,7 +405,8 @@
     begin_sum(1)
     for n, half in parts:
         halo(sbuf, n, s_s, s_r, half).wait_send()
-        halo(dbuf, n, d_s, d_r, half).wait_send()
+    for n, half in quarters:
+        halo(dbuf, n, d_s, d_r, half, 4).wait_send()
     for k in range(4):
         pair(1 - core, k).wait_send()
 
@@ -536,12 +541,12 @@
     vmem = pl.BlockSpec(memory_space=pltpu.VMEM)
     smem = pl.BlockSpec(memory_space=pltpu.SMEM)
     dma = pltpu.SemaphoreType.DMA
-    hbm = pl.BlockSpec(memory_space=pl.ANY)
+    hbm = pl.BlockSpec(memory_space=pltpu.HBM)
     source_gradient, taps = pl.pallas_call(
         kernel,
         out_shape=(
-            jax.ShapeDtypeStruct((8, 64, 128), F32),
-            jax.ShapeDtypeStruct((2, TILES, 64, 128), BF),
+            pltpu.VMEM((8, 64, 128), F32),
+            pltpu.VMEM((2, TILES, 64, 128), BF),
         ),
         in_specs=[hbm, hbm, hbm, hbm, smem],
         out_specs=(vmem, vmem),
@@ -566,13 +571,13 @@
             pltpu.VMEM((3, 256, LANES), BF),
             pltpu.VMEM((256, LANES), F32),
             pltpu.VMEM((64, 128), F32),
-            pltpu.VMEM((1, 128), F32),
+            pltpu.VMEM((1, 256), F32),
             pltpu.VMEM((2, TILES, 64, 128), F32),
             pltpu.VMEM((TILES, 64, 128), F32),
             pltpu.VMEM((TILES, 64, 128), BF),
             pltpu.VMEM((16, 64, 128), BF),
             pltpu.VMEM((8, 64, 128), BF),
-            dma((16,)), dma((16,)), dma((16,)), dma((16,)), dma((4,)), dma((4,)),
+            dma((16,)), dma((16,)), dma((32,)), dma((32,)), dma((4,)), dma((4,)),
             dma((TILES,)), dma((16,)), dma((8,)), dma((8,)),
             dma((16,)), dma((TILES,)), dma((TILES,)), dma((TILES,)),
         ],

time: 56.3 us -> 53.3 us (0.947)
  local copies, waits for them, and re-layouts: 1.96 us -> 0 us
  Pallas kernels: 53.5 us -> 52.5 us
    unnamed x4 -> x0, local copies, waits for them, and re-layouts: 1.96 us -> none
    pallas_call x1, Pallas kernels: 51.5 us -> 50.6 us  [shards(): pl.pallas_call(kernel, out_shape=(pltpu.VMEM((8, 64, 128), F32), pltpu.VM...]
where the time goes in v4:
time: 53.3 us; the launch traced here: 53.2 us
  Pallas kernels  52.5 us (98%)
  between operations  0.64 us (1%)
    pallas_call x1, Pallas kernels, shards(): pl.pallas_call(kernel, out_shape=(pltpu.VMEM((8, 64, 128), F32), pltpu.VM...  50.6 us
    pallas_call x1, Pallas kernels, shards(): pl.pallas_call(unpack, out_shape=(jax.ShapeDtypeStruct((1, 1), F32), jax....  1.96 us

profile of v4, /device:TPU:1, one launch (start us, length us, event | category | flops | bytes accessed | tf_op | source)
XLA Modules:
  0.0 53.2 jit_solution(17192230819516232993)
XLA Ops:
  0.6 50.6 %shard_map.84 = (f32[8,64,128]{2,1,0:T(8,128)S(1)}, bf16[2,14,64,128]{3,2,1,0:T(8,128)(2,1)S(1)}) custom-call(bf16[64,8,128]{2,1,0:T(8,128)(2,1)} %bitcast.15, bf16[27,64,64]{2,1,0:T(8,128)(2,1)} %bitcast.12, bf16[27,64,64]{2,1,0:T(8,128)(2,1)} %bitcast.13, f32[1,64]{1,0:T(1,128)} %bitcast.16, s32[1,8]{1,0:T(1,128)} %lw_ref.1), custom_call_target="tpu_custom_call" | custom-call | flops 3000000000 | bytes 4000000 | tf_op jit(solution)/shard_map/pallas_call | solution.py:545
  51.2 2.0 %shard_map.85 = (f32[1,1]{1,0:T(1,128)}, f32[64,8,128]{2,1,0:T(8,128)}, f32[27,64,64]{2,1,0:T(8,128)}, f32[27,64,64]{2,1,0:T(8,128)}) custom-call(bf16[2,14,64,128]{3,2,1,0:T(8,128)(2,1)S(1)} %get-tuple-element.10.fin, f32[8,64,128]{2,1,0:T(8,128)S(1)} %get-tuple-element.11.sg_ref), custom_call_target="tpu_custom_call" | custom-call | tf_op jit(solution)/shard_map/pallas_call | solution.py:595

commit v5 on v4

--- a/solution.py
+++ b/solution.py
@@ -57,7 +57,7 @@
 def kernel(
     src_hbm, wg_hbm, wc_hbm, ro_hbm, lw_ref,
     sg_ref, fin,
-    src_ref, wg_ref, wc_ref, ro_ref, lsem, half_field, stage, sbuf, dbuf, wg, wgt, wc, wct, u, d, f, slope, dg, q, ro, lossv,
+    src_ref, wg_ref, wc_ref, ro_ref, lsem, rounds, half_field, stage, sbuf, dbuf, wg, wgt, wc, wct, u, d, f, slope, dg, q, ro, lossv,
     part, core_rx, psend, plane_rx, z_rx,
     s_s, s_r, d_s, d_r, c_s, c_r, p_s, p_r, z_s, z_r, g_s, g_r, f_s, f_r,
 ):
@@ -81,14 +81,13 @@
             src_ref=src, dst_ref=dst, send_sem=send, recv_sem=recv, device_id=dev, device_id_type=MESH
         )
 
-    def halo(buf, n, send, recv, half=0, pieces=2):
+    def halo(buf, n, send, recv, quarter=0):
         dx, dy = SIDES[n]
         if dy == 0:
-            count = 8 // pieces
-            here = there = pl.ds(1 + count * half, count)
+            here = there = pl.ds(1 + 2 * quarter, 2)
         else:
             here, there = pl.ds(8 if dy > 0 else 1, 1), pl.ds(0 if dy > 0 else 9, 1)
-        n = n + 8 * half
+        n = n + 8 * quarter
         return rcopy(buf.at[1, here], buf.at[1 - dx, there], send.at[n], recv.at[n], side_dev((dx, dy)))
 
     loads = [
@@ -107,24 +106,34 @@
         greet(side_dev(side))
     greet(core_dev)
 
-    @pl.loop(1, 16)
-    def _(t):
-        greet(plane_dev((pme + t) % 16))
-
-    @pl.loop(1, 8)
-    def _(t):
-        greet(z_dev((z + t) % 8))
+    near = [
+        (gx, ((x + 1) % 4) * 2 + core),
+        (gx, ((x + 3) % 4) * 2 + core),
+        (z * 4 + (y + 1) % 4, gy),
+        (z * 4 + (y + 3) % 4, gy),
+        (((z + 1) % 8) * 4 + y, gy),
+        (((z + 7) % 8) * 4 + y, gy),
+    ]
+    for dev in near:
+        greet(dev)
+
+    def tell(k):
+        for dev in near:
+            pl.semaphore_signal(rounds.at[k], inc=1, device_id=dev, device_id_type=MESH)
+
+    def hear(k):
+        pl.semaphore_wait(rounds.at[k], 6)
 
     loads[0].wait()
     stage[...] = src_ref[...].astype(F32)
     for r in range(8):
         sbuf[1, r + 1] = stage[:, r, :].astype(BF)
 
-    pl.semaphore_wait(barrier, 8 + 1 + 15 + 7)
-    parts = [(n, 0) for n in (4, 5, 6, 7, 2, 3)] + [(n, h) for h in range(2) for n in (0, 1)]
-    quarters = parts[:6] + [(n, h) for h in range(4) for n in (0, 1)]
-    for n, half in parts:
-        halo(sbuf, n, s_s, s_r, half).start()
+    pl.semaphore_wait(barrier, 8 + 1 + 6)
+    parts = [(n, 0) for n in (4, 5, 6, 7, 2, 3)] + [(n, quarter) for quarter in range(4) for n in (0, 1)]
+    for n, quarter in parts:
+        halo(sbuf, n, s_s, s_r, quarter).start()
+    tell(0)
     for load in loads[1:]:
         load.wait()
 
@@ -174,12 +183,13 @@
             put_here(out, xs, r, pair)
             put_below(out, xs, r, pair)
 
-    def arrive(buf, out, send, recv, pieces):
-        count = 8 // pieces
-        for half in range(pieces):
+    def arrive(buf, out, send, recv, rest):
+        for quarter in range(4):
             for n, xs, keep in ((0, 0, None), (1, 2, gx < 31)):
-                halo(buf, n, send, recv, half, pieces).wait_recv()
-                own_rows(buf, out, xs, keep, 1 + count * half, count + count * half)
+                halo(buf, n, send, recv, quarter).wait_recv()
+                own_rows(buf, out, xs, keep, 2 * quarter + 1, 2 * quarter + 2)
+            if quarter:
+                rest(quarter - 1)
         for n in range(2, 8):
             halo(buf, n, send, recv).wait_recv()
         edge_rows(buf, out, 1)
@@ -229,7 +239,15 @@
         f[s, 0:128, 0:128] = jnp.zeros((128, 128), BF)
         dg[s, 0:128, 0:128] = jnp.zeros((128, 128), BF)
 
-    arrive(sbuf, u, s_s, s_r, 2)
+    def fire_rest(j):
+        c = at(j * 2 + 1, 2)
+        low, high = up_rest(wgt, u, c)
+        fire(0, slope[0, :, c] + low, c)
+        fire(2, slope[2, :, c] + high, c)
+
+    arrive(sbuf, u, s_s, s_r, fire_rest)
+    hear(0)
+    tell(1)
 
     for s, v in enumerate(up_low(wgt, u)):
         fire_low(s, v)
@@ -239,12 +257,7 @@
     slope[0, :, c] = low
     slope[2, :, c] = high
 
-    @pl.loop(0, 4)
-    def _(j):
-        c = at(j * 2 + 1, 2)
-        low, high = up_rest(wgt, u, c)
-        fire(0, slope[0, :, c] + low, c)
-        fire(2, slope[2, :, c] + high, c)
+    fire_rest(3)
 
     @pl.when(gx == 0)
     def _():
@@ -295,7 +308,9 @@
         for n in {0: (5, 7, 3), 3: (4, 6, 2)}.get(j, ()):
             halo(dbuf, n, d_s, d_r).start()
         for n in (0, 1):
-            halo(dbuf, n, d_s, d_r, j, 4).start()
+            halo(dbuf, n, d_s, d_r, j).start()
+    hear(1)
+    tell(2)
     own_rows(dbuf, d, 1)
 
     @pl.loop(0, 3)
@@ -373,7 +388,14 @@
     part[0, 13, 0:16, :] = jnp.where(put, loss, part[0, 13, 0:16, :])
     give(0, [3])
 
-    arrive(dbuf, d, d_s, d_r, 4)
+    def back_rest(j):
+        c = at(j * 2 + 1, 2)
+        low, high = up_rest(wc, d, c)
+        dg[0, :, c] = ((half_field[0, :, c] + low) * slope[0, :, c]).astype(BF)
+        dg[2, :, c] = ((half_field[1, :, c] + high) * slope[2, :, c]).astype(BF)
+
+    arrive(dbuf, d, d_s, d_r, back_rest)
+    hear(2)
     begin_sum(0)
 
     for s, v in enumerate(up_low(wc, d)):
@@ -384,12 +406,7 @@
     half_field[0, :, c] = low
     half_field[1, :, c] = high
 
-    @pl.loop(0, 4)
-    def _(j):
-        c = at(j * 2 + 1, 2)
-        low, high = up_rest(wc, d, c)
-        dg[0, :, c] = ((half_field[0, :, c] + low) * slope[0, :, c]).astype(BF)
-        dg[2, :, c] = ((half_field[1, :, c] + high) * slope[2, :, c]).astype(BF)
+    back_rest(3)
 
     clear(u, 1)
     for s in range(3):
@@ -403,10 +420,9 @@
         give(1, [s, 3] if s == 2 else [s])
 
     begin_sum(1)
-    for n, half in parts:
-        halo(sbuf, n, s_s, s_r, half).wait_send()
-    for n, half in quarters:
-        halo(dbuf, n, d_s, d_r, half, 4).wait_send()
+    for n, quarter in parts:
+        halo(sbuf, n, s_s, s_r, quarter).wait_send()
+        halo(dbuf, n, d_s, d_r, quarter).wait_send()
     for k in range(4):
         pair(1 - core, k).wait_send()
 
@@ -556,6 +572,7 @@
             pltpu.VMEM((27, 64, 64), BF),
             pltpu.VMEM((1, 64), F32),
             dma((4,)),
+            pltpu.SemaphoreType.REGULAR((3,)),
             pltpu.VMEM((2, 256, LANES), F32),
             pltpu.VMEM((64, 8, 128), F32),
             pltpu.VMEM((3, 10, 64, 128), BF),
@@ -577,7 +594,7 @@
             pltpu.VMEM((TILES, 64, 128), BF),
             pltpu.VMEM((16, 64, 128), BF),
             pltpu.VMEM((8, 64, 128), BF),
-            dma((16,)), dma((16,)), dma((32,)), dma((32,)), dma((4,)), dma((4,)),
+            dma((32,)), dma((32,)), dma((32,)), dma((32,)), dma((4,)), dma((4,)),
             dma((TILES,)), dma((16,)), dma((8,)), dma((8,)),
             dma((16,)), dma((TILES,)), dma((TILES,)), dma((TILES,)),
         ],

time: 53.3 us -> 50.7 us (0.951)
  Pallas kernels: 52.5 us -> 49.9 us
    pallas_call x1, Pallas kernels: 50.6 us -> 48 us  [shards(): pl.pallas_call(kernel, out_shape=(pltpu.VMEM((8, 64, 128), F32), pltpu.VM...]
where the time goes in v5:
time: 50.7 us; the launch traced here: 50.6 us
  Pallas kernels  49.9 us (98%)
  between operations  0.64 us (1%)
    pallas_call x1, Pallas kernels, shards(): pl.pallas_call(kernel, out_shape=(pltpu.VMEM((8, 64, 128), F32), pltpu.VM...  48 us
    pallas_call x1, Pallas kernels, shards(): pl.pallas_call(unpack, out_shape=(jax.ShapeDtypeStruct((1, 1), F32), jax....  1.96 us

profile of v5, /device:TPU:1, one launch (start us, length us, event | category | flops | bytes accessed | tf_op | source)
XLA Modules:
  0.0 50.6 jit_solution(538784218307684462)
XLA Ops:
  0.6 48.0 %shard_map.84 = (f32[8,64,128]{2,1,0:T(8,128)S(1)}, bf16[2,14,64,128]{3,2,1,0:T(8,128)(2,1)S(1)}) custom-call(bf16[64,8,128]{2,1,0:T(8,128)(2,1)} %bitcast.15, bf16[27,64,64]{2,1,0:T(8,128)(2,1)} %bitcast.12, bf16[27,64,64]{2,1,0:T(8,128)(2,1)} %bitcast.13, f32[1,64]{1,0:T(1,128)} %bitcast.16, s32[1,8]{1,0:T(1,128)} %lw_ref.1), custom_call_target="tpu_custom_call" | custom-call | flops 3000000000 | bytes 4000000 | tf_op jit(solution)/shard_map/pallas_call | solution.py:561
  48.6 2.0 %shard_map.85 = (f32[1,1]{1,0:T(1,128)}, f32[64,8,128]{2,1,0:T(8,128)}, f32[27,64,64]{2,1,0:T(8,128)}, f32[27,64,64]{2,1,0:T(8,128)}) custom-call(bf16[2,14,64,128]{3,2,1,0:T(8,128)(2,1)S(1)} %get-tuple-element.10.fin, f32[8,64,128]{2,1,0:T(8,128)S(1)} %get-tuple-element.11.sg_ref), custom_call_target="tpu_custom_call" | custom-call | tf_op jit(solution)/shard_map/pallas_call | solution.py:612

commit v6 on v5

--- a/solution.py
+++ b/solution.py
@@ -15,6 +15,13 @@
 TILES = 14
 TAP = {(0, 0): 1, (1, 0): 2, (1, 1): 0}
 SIDES = [(1, 0), (-1, 0), (0, 1), (0, -1), (1, 1), (1, -1), (-1, 1), (-1, -1)]
+
+
+AWAY = sorted(
+    ((a, b) for a in range(4) for b in range(4) if a or b),
+    key=lambda step: -min(step[0], 4 - step[0]) - min(step[1], 4 - step[1]),
+)
+AWAY_Z = (4, 3, 5, 2, 6, 1, 7)
 
 
 def dot(a, b):
@@ -335,6 +342,9 @@
     def loss_tile(t):
         return jnp.logical_and(core == 0, t == 13)
 
+    def other(step):
+        return ((x + step[0]) % 4) * 4 + (y + step[1]) % 4
+
     def to_owner(dst, src):
         return rcopy(psend.at[dst], plane_rx.at[src], p_s.at[dst], p_r.at[src], plane_dev(dst))
 
@@ -344,22 +354,25 @@
             for k in range(4):
                 pair(g, k).wait_recv()
 
-            @pl.loop(1, 17)
-            def _(i):
-                t = (pme + i) % 16
+            def ready(t):
+                total = part[g, t] + core_rx[t]
+                psend[t] = total.astype(BF)
+                if g == 0:
+                    @pl.when(t == 13)
+                    def _():
+                        psend[t] = split_round(total)
+
+            for step in AWAY:
+                t = other(step)
 
                 @pl.when(t < TILES)
                 def _():
-                    total = part[g, t] + core_rx[t]
-                    psend[t] = total.astype(BF)
-                    if g == 0:
-                        @pl.when(t == 13)
-                        def _():
-                            psend[t] = split_round(total)
-
-                    @pl.when(t != pme)
-                    def _():
-                        to_owner(t, pme).start()
+                    ready(t)
+                    to_owner(t, pme).start()
+
+            @pl.when(pme < TILES)
+            def _():
+                ready(pme)
 
     def pack(g, s, full, halves):
         for j in range(3):
@@ -462,8 +475,7 @@
         def _():
             z_rx[z] = split_round(total)
 
-        @pl.loop(1, 8)
-        def _(i):
+        for i in AWAY_Z:
             along_z((z + i) % 8, z).start()
 
         @pl.loop(1, 8)
@@ -481,9 +493,8 @@
             fin[core, pme] = split_round(total)
 
 
-        @pl.loop(1, 16)
-        def _(i):
-            to_plane((pme + i) % 16, pme).start()
+        for step in AWAY:
+            to_plane(other(step), pme).start()
 
         to_core(core, pme).start()
 

time: 50.7 us -> 49.3 us (0.972)
  Pallas kernels: 49.9 us -> 48.5 us
    pallas_call x1, Pallas kernels: 48 us -> 46.6 us  [shards(): pl.pallas_call(kernel, out_shape=(pltpu.VMEM((8, 64, 128), F32), pltpu.VM...]
where the time goes in v6:
time: 49.3 us; the launch traced here: 49.2 us
  Pallas kernels  48.5 us (98%)
  between operations  0.64 us (1%)
    pallas_call x1, Pallas kernels, shards(): pl.pallas_call(kernel, out_shape=(pltpu.VMEM((8, 64, 128), F32), pltpu.VM...  46.6 us
    pallas_call x1, Pallas kernels, shards(): pl.pallas_call(unpack, out_shape=(jax.ShapeDtypeStruct((1, 1), F32), jax....  1.96 us

profile of v6, /device:TPU:1, one launch (start us, length us, event | category | flops | bytes accessed | tf_op | source)
XLA Modules:
  0.0 49.2 jit_solution(11844499585426720575)
XLA Ops:
  0.6 46.6 %shard_map.84 = (f32[8,64,128]{2,1,0:T(8,128)S(1)}, bf16[2,14,64,128]{3,2,1,0:T(8,128)(2,1)S(1)}) custom-call(bf16[64,8,128]{2,1,0:T(8,128)(2,1)} %bitcast.15, bf16[27,64,64]{2,1,0:T(8,128)(2,1)} %bitcast.12, bf16[27,64,64]{2,1,0:T(8,128)(2,1)} %bitcast.13, f32[1,64]{1,0:T(1,128)} %bitcast.16, s32[1,8]{1,0:T(1,128)} %lw_ref.1), custom_call_target="tpu_custom_call" | custom-call | flops 3000000000 | bytes 4000000 | tf_op jit(solution)/shard_map/pallas_call | solution.py:572
  47.2 2.0 %shard_map.85 = (f32[1,1]{1,0:T(1,128)}, f32[64,8,128]{2,1,0:T(8,128)}, f32[27,64,64]{2,1,0:T(8,128)}, f32[27,64,64]{2,1,0:T(8,128)}) custom-call(bf16[2,14,64,128]{3,2,1,0:T(8,128)(2,1)S(1)} %get-tuple-element.10.fin, f32[8,64,128]{2,1,0:T(8,128)S(1)} %get-tuple-element.11.sg_ref), custom_call_target="tpu_custom_call" | custom-call | tf_op jit(solution)/shard_map/pallas_call | solution.py:623

commit v7 on v6

--- a/solution.py
+++ b/solution.py
@@ -109,7 +109,7 @@
     def greet(dev):
         pl.semaphore_signal(barrier, inc=1, device_id=dev, device_id_type=MESH)
 
-    for side in SIDES:
+    for side in SIDES[4:] + SIDES[:4]:
         greet(side_dev(side))
     greet(core_dev)
 
@@ -409,7 +409,6 @@
 
     arrive(dbuf, d, d_s, d_r, back_rest)
     hear(2)
-    begin_sum(0)
 
     for s, v in enumerate(up_low(wc, d)):
         dg[s, 128:256, 0:128] = (v * slope[s, 128:256, 0:128]).astype(BF)
@@ -432,6 +431,7 @@
         )
         give(1, [s, 3] if s == 2 else [s])
 
+    begin_sum(0)
     begin_sum(1)
     for n, quarter in parts:
         halo(sbuf, n, s_s, s_r, quarter).wait_send()
@@ -459,15 +459,10 @@
 
     @pl.when(pme < TILES)
     def _():
-        plane_rx[pme] = psend[pme]
-
-        @pl.loop(1, 16)
-        def _(i):
-            t = (pme + i) % 16
+        total = psend[pme].astype(F32)
+        for step in AWAY[::-1]:
+            t = other(step)
             to_owner(pme, t).wait_recv()
-
-        total = plane_rx[0].astype(F32)
-        for t in range(1, 16):
             total += plane_rx[t].astype(F32)
         z_rx[z] = total.astype(BF)
 

time: 49.3 us -> 52.4 us (1.063)
  Pallas kernels: 48.5 us -> 51.6 us
    pallas_call x1, Pallas kernels: 46.6 us -> 49.7 us  [shards(): pl.pallas_call(kernel, out_shape=(pltpu.VMEM((8, 64, 128), F32), pltpu.VM...]
where the time goes in v7:
time: 52.4 us; the launch traced here: 52.3 us
  Pallas kernels  51.6 us (98%)
  between operations  0.64 us (1%)
    pallas_call x1, Pallas kernels, shards(): pl.pallas_call(kernel, out_shape=(pltpu.VMEM((8, 64, 128), F32), pltpu.VM...  49.7 us
    pallas_call x1, Pallas kernels, shards(): pl.pallas_call(unpack, out_shape=(jax.ShapeDtypeStruct((1, 1), F32), jax....  1.96 us

profile of v7, /device:TPU:1, one launch (start us, length us, event | category | flops | bytes accessed | tf_op | source)
XLA Modules:
  0.0 52.3 jit_solution(17152051672175053817)
XLA Ops:
  0.6 49.7 %shard_map.84 = (f32[8,64,128]{2,1,0:T(8,128)S(1)}, bf16[2,14,64,128]{3,2,1,0:T(8,128)(2,1)S(1)}) custom-call(bf16[64,8,128]{2,1,0:T(8,128)(2,1)} %bitcast.15, bf16[27,64,64]{2,1,0:T(8,128)(2,1)} %bitcast.12, bf16[27,64,64]{2,1,0:T(8,128)(2,1)} %bitcast.13, f32[1,64]{1,0:T(1,128)} %bitcast.16, s32[1,8]{1,0:T(1,128)} %lw_ref.1), custom_call_target="tpu_custom_call" | custom-call | flops 3000000000 | bytes 4000000 | tf_op jit(solution)/shard_map/pallas_call | solution.py:567
  50.3 2.0 %shard_map.85 = (f32[1,1]{1,0:T(1,128)}, f32[64,8,128]{2,1,0:T(8,128)}, f32[27,64,64]{2,1,0:T(8,128)}, f32[27,64,64]{2,1,0:T(8,128)}) custom-call(bf16[2,14,64,128]{3,2,1,0:T(8,128)(2,1)S(1)} %get-tuple-element.10.fin, f32[8,64,128]{2,1,0:T(8,128)S(1)} %get-tuple-element.11.sg_ref), custom_call_target="tpu_custom_call" | custom-call | tf_op jit(solution)/shard_map/pallas_call | solution.py:618
